TPU v7x, 128 devices: a whole 4x4x4 slice. The times are simulated.
128 devices in a mesh: fsdp: 32 (over x, z, core), dp: 4 (over y).
Axes of the slice: x: 4, y: 4, z: 4, core: 2. Of those that a mesh axis runs over, the one named last changes fastest.
Arguments:
- tokens_in: bfloat16 [2, 32768, 640], P(None, ('fsdp', 'dp')), may hold values from -6 to 6
- cotangent: bfloat16 [2, 32768, 640], P(None, ('fsdp', 'dp')), may hold values from -6 to 6
- doc_lengths: int32 [32, 2, 3], P('fsdp'), may hold values from 1 to 960, 1024 in all within a row
- w_query: bfloat16 [640, 1024], P(('fsdp', 'dp')), may hold values from -0.25 to 0.25
- w_key: bfloat16 [640, 256], P(('fsdp', 'dp')), may hold values from -0.25 to 0.25
- w_value: bfloat16 [640, 256], P(('fsdp', 'dp')), may hold values from -0.25 to 0.25
- w_out: bfloat16 [1024, 640], P(('fsdp', 'dp')), may hold values from -0.1875 to 0.1875
- gain_attn_in: bfloat16 [640], P(('fsdp', 'dp')), may hold values from 0.099609375 to 1.8984375
- gain_attn_out: bfloat16 [640], P(('fsdp', 'dp')), may hold values from 0.099609375 to 1.8984375
- gain_query: bfloat16 [256], P(('fsdp', 'dp')), may hold values from 0.099609375 to 1.8984375
- gain_key: bfloat16 [256], P(('fsdp', 'dp')), may hold values from 0.099609375 to 1.8984375
- w_gate: bfloat16 [640, 2048], P(('fsdp', 'dp')), may hold values from -0.25 to 0.25
- w_up: bfloat16 [640, 2048], P(('fsdp', 'dp')), may hold values from -0.25 to 0.25
- w_down: bfloat16 [2048, 640], P(('fsdp', 'dp')), may hold values from -0.125 to 0.125
- gain_ffn_in: bfloat16 [640], P(('fsdp', 'dp')), may hold values from 0.099609375 to 1.8984375
- gain_ffn_out: bfloat16 [640], P(('fsdp', 'dp')), may hold values from 0.099609375 to 1.8984375
Outputs:
- layer_out: bfloat16 [2, 32768, 640], P(None, ('fsdp', 'dp'))
- grad_tokens: float32 [2, 32768, 640], P(None, ('fsdp', 'dp'))
- grad_query: float32 [640, 1024], P(('fsdp', 'dp'))
- grad_key: float32 [640, 256], P(('fsdp', 'dp'))
- grad_value: float32 [640, 256], P(('fsdp', 'dp'))
- grad_out: float32 [1024, 640], P(('fsdp', 'dp'))
- grad_attn_in: float32 [640], P(('fsdp', 'dp'))
- grad_attn_out: float32 [640], P(('fsdp', 'dp'))
- grad_gain_query: float32 [256], P(('fsdp', 'dp'))
- grad_gain_key: float32 [256], P(('fsdp', 'dp'))
- grad_gate: float32 [640, 2048], P(('fsdp', 'dp'))
- grad_up: float32 [640, 2048], P(('fsdp', 'dp'))
- grad_down: float32 [2048, 640], P(('fsdp', 'dp'))
- grad_ffn_in: float32 [640], P(('fsdp', 'dp'))
- grad_ffn_out: float32 [640], P(('fsdp', 'dp'))
Inputs may be any that keep to these rules, and one draw needn't show every extreme that they name: `doc_lengths`: each row of 3 lengths sums to 1024; its largest is exactly 960.
All inputs are finite; a program needn't handle non-finite values.
Results may differ from a plain program's by a relative error of at most 0.035.
Values may be sent and summed in bfloat16 or wider, within the bound.
A program may use at most 192 MiB of HBM per device.

v0:
```python
import math

import jax
import jax.numpy as jnp
from jax import lax
from jax.sharding import PartitionSpec as P

HEADS = 4
HEAD_DIM = 256


norm_eps = 1e-06
rope_base = 1000000.0
masked_fill = -1e30


def side_by_side(arrays, axis, dim, along):
    ends, at = ([], 0)
    for a in arrays[:-1]:
        at += a.shape[along]
        ends.append(at)
    both = jnp.concatenate(arrays, axis=along)
    return tuple(jnp.split(lax.all_gather(both, axis, axis=dim, tiled=True), ends, axis=along))


def split_up(array, dim, peers):
    dims = array.shape
    blocks = array.reshape(*dims[:dim], peers, dims[dim] // peers, *dims[dim + 1 :])
    return jnp.moveaxis(blocks, dim, 0)


def sum_at_owner(array, axis, dim):
    peers = lax.axis_size(axis)
    blocks = lax.all_to_all(split_up(array, dim, peers), axis, 0, 0, tiled=True)
    return jnp.sum(blocks.astype(jnp.float32), axis=0)


def sent_together(arrays, axis, dim, along):
    widths = [a.shape[along] for a in arrays]
    both = jnp.concatenate(arrays, axis=along)
    result = sum_at_owner(both, axis, dim)
    return tuple(jnp.split(result, [sum(widths[:k]) for k in range(1, len(widths))], axis=along))


def one_scatter(arrays, axis, dims):
    peers = lax.axis_size(axis)
    blocks = [split_up(a, dim, peers) for a, dim in zip(arrays, dims)]
    lines = jnp.concatenate([b.reshape(peers, -1) for b in blocks], axis=1)
    span = max(16, -(-lines.shape[1] // 1024) * 8)
    lines = jnp.pad(lines, ((0, 0), (0, span * 128 - lines.shape[1]))).reshape(-1, 128)
    line, at, outs = (lax.psum_scatter(lines, axis, tiled=True).reshape(-1), 0, [])
    for b in blocks:
        part = b[0]
        outs.append(line[at : at + part.size].reshape(part.shape))
        at += part.size
    return tuple(outs)


def rms_scale(value_in, gain_in):
    return (
        value_in * lax.rsqrt(jnp.mean(value_in * value_in, -1, keepdims=True) + norm_eps) * gain_in
    )


def rotate(value_in, cosine, sine_part):
    half_width = value_in.shape[-1] // 2
    first_half = value_in[..., :half_width]
    second_half = value_in[..., half_width:]
    return jnp.concatenate(
        [
            first_half * cosine - second_half * sine_part,
            second_half * cosine + first_half * sine_part,
        ],
        -1,
    )


def angles(places, feat_width):
    half_width = feat_width // 2
    inv_freq = jnp.exp(
        jnp.arange(half_width, dtype=jnp.float32) * (-2.0 * math.log(rope_base) / feat_width)
    )
    turned = places.astype(jnp.float32)[:, None] * inv_freq[None, :]
    return (jnp.cos(turned), jnp.sin(turned))


def doc_layout(lengths, group_rows):
    doc_ends = jnp.cumsum(lengths)
    order_ids = jnp.arange(group_rows, dtype=jnp.int32)
    passed = (order_ids[:, None] >= doc_ends[None, :]).astype(jnp.int32)
    doc_ids = jnp.sum(passed, 1)
    starts = jnp.sum(passed * lengths[None, :], 1)
    return (doc_ids, order_ids - starts)


def add_into(totals, terms):
    if totals is None:
        return terms
    return tuple((total_v + term_v for total_v, term_v in zip(totals, terms)))


def glu_mix(gate_proj, up_proj):
    return jax.nn.gelu(gate_proj, approximate=True) * up_proj


def on_device(
    tokens_in,
    cotangent,
    doc_lengths,
    w_query,
    w_key,
    w_value,
    w_out,
    gain_attn_in,
    gain_attn_out,
    gain_query,
    gain_key,
    w_gate,
    w_up,
    w_down,
    gain_ffn_in,
    gain_ffn_out,
):
    micro_count, tok_rows, feat_width = tokens_in.shape
    dp_index = lax.axis_index("dp")
    group_rows = lax.axis_size("dp") * tok_rows
    soft_scale = HEAD_DIM ** (-0.5)
    f32 = jnp.float32
    bf16 = jnp.bfloat16
    order_all = jnp.arange(group_rows, dtype=jnp.int32)
    own_order = dp_index * tok_rows + jnp.arange(tok_rows, dtype=jnp.int32)
    attn_total = None
    ffn_total = None
    layer_rows = []
    input_grads = []
    for micro_idx in range(micro_count):
        attn_full = (
            *side_by_side((w_query, w_key, w_value), ("fsdp", "dp"), 0, 1),
            lax.all_gather(w_out, ("fsdp", "dp"), axis=0, tiled=True),
            lax.all_gather(gain_attn_in, ("fsdp", "dp"), axis=0, tiled=True),
            lax.all_gather(gain_attn_out, ("fsdp", "dp"), axis=0, tiled=True),
            lax.all_gather(gain_query, ("fsdp", "dp"), axis=0, tiled=True),
            lax.all_gather(gain_key, ("fsdp", "dp"), axis=0, tiled=True),
        )
        (
            query_full,
            key_full,
            value_full,
            out_full,
            attn_in_b,
            attn_out_b,
            query_gain_b,
            key_gain_b,
        ) = attn_full
        attn_in_gain = attn_in_b.astype(f32)
        attn_out_gain = attn_out_b.astype(f32)
        query_gain = query_gain_b.astype(f32)
        key_gain = key_gain_b.astype(f32)
        x_now = tokens_in[micro_idx].astype(f32)
        doc_ids, places = doc_layout(doc_lengths[0, micro_idx], group_rows)
        own_docs = lax.dynamic_slice_in_dim(doc_ids, dp_index * tok_rows, tok_rows)
        own_places = lax.dynamic_slice_in_dim(places, dp_index * tok_rows, tok_rows)
        visible = (own_docs[:, None] == doc_ids[None, :]) & (
            own_order[:, None] >= order_all[None, :]
        )
        cosine, sine_part = angles(own_places, HEAD_DIM)
        cos_heads = cosine[:, None, :]
        sin_heads = sine_part[:, None, :]

        def query_path(value_in, gain_in):
            return rotate(rms_scale(value_in, gain_in), cos_heads, sin_heads)

        def key_path(value_in, gain_in):
            return rotate(rms_scale(value_in, gain_in), cosine, sine_part)

        normed = rms_scale(x_now, attn_in_gain).astype(bf16)
        query_raw = jnp.dot(normed, query_full, preferred_element_type=f32).reshape(
            tok_rows, HEADS, HEAD_DIM
        )
        key_raw = jnp.dot(normed, key_full, preferred_element_type=f32)
        queries = query_path(query_raw, query_gain).astype(bf16)
        keys_own = key_path(key_raw, key_gain).astype(bf16)
        values_own = jnp.dot(normed, value_full, preferred_element_type=f32).astype(bf16)
        keys_all, values_all = (
            lax.all_gather(keys_own, "dp", axis=0, tiled=True),
            lax.all_gather(values_own, "dp", axis=0, tiled=True),
        )
        scores = (
            jnp.einsum("thd,sd->hts", queries, keys_all, preferred_element_type=f32) * soft_scale
        )
        scores = jnp.where(visible[None], scores, masked_fill)
        row_max = jnp.max(scores, -1, keepdims=True)
        scaled_exp = jnp.exp(scores - row_max)
        row_total = jnp.sum(scaled_exp, -1, keepdims=True)
        attn_probs = scaled_exp / row_total
        log_total = row_max + jnp.log(row_total)
        attn_mix = jnp.einsum(
            "hts,sd->thd", attn_probs.astype(bf16), values_all, preferred_element_type=f32
        )
        attn_mix = attn_mix.reshape(tok_rows, HEADS * HEAD_DIM).astype(bf16)
        branch = jnp.dot(attn_mix, out_full, preferred_element_type=f32)
        hidden = x_now + rms_scale(branch, attn_out_gain)
        ffn_full = (
            *side_by_side((w_gate, w_up), ("fsdp", "dp"), 0, 1),
            lax.all_gather(w_down, ("fsdp", "dp"), axis=0, tiled=True),
            lax.all_gather(gain_ffn_in, ("fsdp", "dp"), axis=0, tiled=True),
            lax.all_gather(gain_ffn_out, ("fsdp", "dp"), axis=0, tiled=True),
        )
        gate_full, up_full, down_full, ffn_in_b, ffn_out_b = ffn_full
        normed_ffn = rms_scale(hidden, ffn_in_b.astype(f32)).astype(bf16)
        gate_proj = jnp.dot(normed_ffn, gate_full, preferred_element_type=f32)
        up_proj = jnp.dot(normed_ffn, up_full, preferred_element_type=f32)
        hidden_mix = glu_mix(gate_proj, up_proj).astype(bf16)
        down_proj = jnp.dot(hidden_mix, down_full, preferred_element_type=f32)
        layer_rows.append((hidden + rms_scale(down_proj, ffn_out_b.astype(f32))).astype(bf16))
        grad_now = cotangent[micro_idx].astype(f32)
        ffn_back = (
            *side_by_side((w_gate, w_up), ("fsdp", "dp"), 0, 1),
            lax.all_gather(w_down, ("fsdp", "dp"), axis=0, tiled=True),
            lax.all_gather(gain_ffn_in, ("fsdp", "dp"), axis=0, tiled=True),
            lax.all_gather(gain_ffn_out, ("fsdp", "dp"), axis=0, tiled=True),
        )
        gate_back, up_back, down_back, ffn_in_back, ffn_out_back = ffn_back
        unused_out, post_pull = jax.vjp(rms_scale, down_proj, ffn_out_back.astype(f32))
        grad_down_proj, grad_ffn_out_gain = post_pull(grad_now)
        grad_down_b = grad_down_proj.astype(bf16)
        grad_down_w = jnp.einsum("tf,td->fd", hidden_mix, grad_down_b, preferred_element_type=f32)
        grad_mix = jnp.einsum("td,fd->tf", grad_down_b, down_back, preferred_element_type=f32)
        unused_mix, glu_pull = jax.vjp(glu_mix, gate_proj, up_proj)
        grad_gate_proj, grad_up_proj = glu_pull(grad_mix)
        grad_gate_b = grad_gate_proj.astype(bf16)
        grad_up_b = grad_up_proj.astype(bf16)
        grad_gate_w = jnp.einsum("tc,tf->cf", normed_ffn, grad_gate_b, preferred_element_type=f32)
        grad_up_w = jnp.einsum("tc,tf->cf", normed_ffn, grad_up_b, preferred_element_type=f32)
        grad_normed_ffn = jnp.einsum(
            "tf,cf->tc", grad_gate_b, gate_back, preferred_element_type=f32
        )
        grad_normed_ffn = grad_normed_ffn + jnp.einsum(
            "tf,cf->tc", grad_up_b, up_back, preferred_element_type=f32
        )
        unused_pre, pre_pull = jax.vjp(rms_scale, hidden, ffn_in_back.astype(f32))
        grad_hidden_part, grad_ffn_in_gain = pre_pull(grad_normed_ffn)
        grad_hidden = grad_now + grad_hidden_part
        ffn_total = add_into(
            ffn_total, (grad_gate_w, grad_up_w, grad_down_w, grad_ffn_in_gain, grad_ffn_out_gain)
        )
        attn_back = (
            *side_by_side((w_query, w_key, w_value), ("fsdp", "dp"), 0, 1),
            lax.all_gather(w_out, ("fsdp", "dp"), axis=0, tiled=True),
            lax.all_gather(gain_attn_in, ("fsdp", "dp"), axis=0, tiled=True),
            lax.all_gather(gain_attn_out, ("fsdp", "dp"), axis=0, tiled=True),
            lax.all_gather(gain_query, ("fsdp", "dp"), axis=0, tiled=True),
            lax.all_gather(gain_key, ("fsdp", "dp"), axis=0, tiled=True),
        )
        (
            query_back,
            key_back,
            value_back,
            out_back,
            attn_in_back,
            attn_out_back,
            query_gain_back,
            key_gain_back,
        ) = attn_back
        unused_branch, branch_pull = jax.vjp(rms_scale, branch, attn_out_back.astype(f32))
        grad_branch, grad_attn_out_gain = branch_pull(grad_hidden)
        grad_branch_b = grad_branch.astype(bf16)
        grad_out_w = jnp.einsum("tc,td->cd", attn_mix, grad_branch_b, preferred_element_type=f32)
        grad_attn_mix = jnp.einsum("td,cd->tc", grad_branch_b, out_back, preferred_element_type=f32)
        grad_attn_mix = grad_attn_mix.reshape(tok_rows, HEADS, HEAD_DIM).astype(bf16)
        scores_again = (
            jnp.einsum("thd,sd->hts", queries, keys_all, preferred_element_type=f32) * soft_scale
        )
        scores_again = jnp.where(visible[None], scores_again, masked_fill)
        probs_again = jnp.exp(scores_again - log_total)
        grad_probs = jnp.einsum(
            "thd,sd->hts", grad_attn_mix, values_all, preferred_element_type=f32
        )
        row_inner = jnp.sum(probs_again * grad_probs, -1, keepdims=True)
        grad_scores = (probs_again * (grad_probs - row_inner)).astype(bf16)
        grad_queries = (
            jnp.einsum("hts,sd->thd", grad_scores, keys_all, preferred_element_type=f32)
            * soft_scale
        )
        grad_keys_part = (
            jnp.einsum("hts,thd->sd", grad_scores, queries, preferred_element_type=f32) * soft_scale
        )
        grad_values_part = jnp.einsum(
            "hts,thd->sd", probs_again.astype(bf16), grad_attn_mix, preferred_element_type=f32
        )
        grad_keys_own, grad_values_own = sent_together(
            (grad_keys_part.astype(jnp.bfloat16), grad_values_part.astype(jnp.bfloat16)), "dp", 0, 1
        )
        unused_key, key_pull = jax.vjp(key_path, key_raw, key_gain_back.astype(f32))
        grad_key_raw, grad_key_gain = key_pull(grad_keys_own)
        unused_query, query_pull = jax.vjp(query_path, query_raw, query_gain_back.astype(f32))
        grad_query_raw, grad_query_gain = query_pull(grad_queries)
        grad_query_b = grad_query_raw.reshape(tok_rows, HEADS * HEAD_DIM).astype(bf16)
        grad_key_b = grad_key_raw.astype(bf16)
        grad_value_b = grad_values_own.astype(bf16)
        grad_query_w = jnp.einsum("tc,tf->cf", normed, grad_query_b, preferred_element_type=f32)
        grad_key_w = jnp.einsum("tc,tf->cf", normed, grad_key_b, preferred_element_type=f32)
        grad_value_w = jnp.einsum("tc,tf->cf", normed, grad_value_b, preferred_element_type=f32)
        grad_normed = jnp.einsum("tf,cf->tc", grad_query_b, query_back, preferred_element_type=f32)
        grad_normed = grad_normed + jnp.einsum(
            "tf,cf->tc", grad_key_b, key_back, preferred_element_type=f32
        )
        grad_normed = grad_normed + jnp.einsum(
            "tf,cf->tc", grad_value_b, value_back, preferred_element_type=f32
        )
        unused_in, in_pull = jax.vjp(rms_scale, x_now, attn_in_back.astype(f32))
        grad_x_part, grad_attn_in_gain = in_pull(grad_normed)
        input_grads.append(grad_hidden + grad_x_part)
        attn_total = add_into(
            attn_total,
            (
                grad_query_w,
                grad_key_w,
                grad_value_w,
                grad_out_w,
                grad_attn_in_gain,
                grad_attn_out_gain,
                grad_query_gain,
                grad_key_gain,
            ),
        )
    ffn_grads = one_scatter(
        (ffn_total[0], ffn_total[1], ffn_total[2], ffn_total[3], ffn_total[4]),
        ("fsdp", "dp"),
        (0, 0, 0, 0, 0),
    )
    attn_grads = (
        lax.psum_scatter(attn_total[0], ("fsdp", "dp"), scatter_dimension=0, tiled=True),
        lax.psum_scatter(attn_total[1], ("fsdp", "dp"), scatter_dimension=0, tiled=True),
        lax.psum_scatter(attn_total[2], ("fsdp", "dp"), scatter_dimension=0, tiled=True),
        lax.psum_scatter(attn_total[3], ("fsdp", "dp"), scatter_dimension=0, tiled=True),
        lax.psum_scatter(attn_total[4], ("fsdp", "dp"), scatter_dimension=0, tiled=True),
        lax.psum_scatter(attn_total[5], ("fsdp", "dp"), scatter_dimension=0, tiled=True),
        lax.psum_scatter(attn_total[6], ("fsdp", "dp"), scatter_dimension=0, tiled=True),
        lax.psum_scatter(attn_total[7], ("fsdp", "dp"), scatter_dimension=0, tiled=True),
    )
    layer_out = jnp.stack(layer_rows)
    grad_tokens = jnp.stack(input_grads)
    return (
        layer_out,
        grad_tokens,
        attn_grads[0],
        attn_grads[1],
        attn_grads[2],
        attn_grads[3],
        attn_grads[4],
        attn_grads[5],
        attn_grads[6],
        attn_grads[7],
        ffn_grads[0],
        ffn_grads[1],
        ffn_grads[2],
        ffn_grads[3],
        ffn_grads[4],
    )


def solution(mesh):
    placed = (
        P(None, ("fsdp", "dp"), None),
        P(None, ("fsdp", "dp"), None),
        P("fsdp", None, None),
        P(("fsdp", "dp"), None),
        P(("fsdp", "dp"), None),
        P(("fsdp", "dp"), None),
        P(("fsdp", "dp"), None),
        P(("fsdp", "dp")),
        P(("fsdp", "dp")),
        P(("fsdp", "dp")),
        P(("fsdp", "dp")),
        P(("fsdp", "dp"), None),
        P(("fsdp", "dp"), None),
        P(("fsdp", "dp"), None),
        P(("fsdp", "dp")),
        P(("fsdp", "dp")),
    )
    return jax.shard_map(
        on_device,
        mesh=mesh,
        in_specs=placed,
        out_specs=(
            P(None, ("fsdp", "dp"), None),
            P(None, ("fsdp", "dp"), None),
            P(("fsdp", "dp"), None),
            P(("fsdp", "dp"), None),
            P(("fsdp", "dp"), None),
            P(("fsdp", "dp"), None),
            P(("fsdp", "dp")),
            P(("fsdp", "dp")),
            P(("fsdp", "dp")),
            P(("fsdp", "dp")),
            P(("fsdp", "dp"), None),
            P(("fsdp", "dp"), None),
            P(("fsdp", "dp"), None),
            P(("fsdp", "dp")),
            P(("fsdp", "dp")),
        ),
        check_vma=False,
    )
```

profile of v0, /device:TPU:1, one launch (start us, length us, event | category | flops | bytes accessed | tf_op | source)
XLA Modules:
  0.0 707.3 jit_solution(4585565102912411561)
XLA Ops:
  16.6 69.6 %all-reduce.26 = (bf16[640]{0:T(1024)(128)(2,1)S(1)}, bf16[256]{0:T(256)(128)(2,1)S(1)}, bf16[256]{0:T(256)(128)(2,1)S(1)}, bf16[640]{0:T(1024)(128)(2,1)S(1)}, ...) all-reduce(bf16[640]{0:T(1024)(128)(2,1)S(1)} %dynamic-update-slice, ...), channel_id=1, replica_groups=mesh['fsdp'=32,'dp'=4] {'fsdp','dp'}, use_global_device_ids=true, to_apply=%add.9 | all-reduce | flops 3072 | bytes 12288
  100.2 10.9 %all_gather.30 = bf16[1024,256]{1,0:T(8,128)(2,1)} all-gather(bf16[256,256]{1,0:T(8,128)(2,1)S(1)} %convolution_convert_fusion.3), channel_id=1, replica_groups=mesh['fsdp'=32,'dp'=4] {'dp'}, dimensions={0}, use_global_device_ids=true | all-gather | bytes 655360 | tf_op jit(solution)/shard_map/all_gather | solution.py:186
  111.1 10.8 %all_gather.40 = bf16[1024,256]{1,0:T(8,128)(2,1)S(1)} all-gather(bf16[256,256]{1,0:T(8,128)(2,1)S(1)} %convolution_convert_fusion.2), channel_id=1, replica_groups=mesh['fsdp'=32,'dp'=4] {'dp'}, dimensions={0}, use_global_device_ids=true | all-gather | bytes 655360 | tf_op jit(solution)/shard_map/all_gather | solution.py:186
  123.3 10.9 %all_gather.41 = bf16[1024,256]{0,1:T(8,128)(2,1)S(1)} all-gather(bf16[256,256]{0,1:T(8,128)(2,1)S(1)} %pad_maximum_fusion.11), channel_id=1, replica_groups=mesh['fsdp'=32,'dp'=4] {'dp'}, dimensions={0}, use_global_device_ids=true | all-gather | bytes 655360 | tf_op jit(solution)/shard_map/all_gather | solution.py:185
  139.1 6.2 all-gather.7.cloned.1.call-done
  147.4 11.5 %all_gather.32 = bf16[1024,256]{0,1:T(8,128)(2,1)S(1)} all-gather(bf16[256,256]{0,1:T(8,128)(2,1)S(1)} %pad_maximum_fusion.10), channel_id=1, replica_groups=mesh['fsdp'=32,'dp'=4] {'dp'}, dimensions={0}, use_global_device_ids=true | all-gather | bytes 655360 | tf_op jit(solution)/shard_map/all_gather | solution.py:185
  165.9 51.0 %all-gather.13.cloned.1.call-done = bf16[128,5,4096]{2,1,0:T(8,128)(2,1)} async-done(((bf16[1,5,4096]{2,1,0:T(8,128)(2,1)}), bf16[128,5,4096]{2,1,0:T(8,128)(2,1)}) %all-gather.13.cloned.1.call-update) | async-done | bytes 5242896 | tf_op jit(solution)/shard_map/all_gather | solution.py:23
  217.0 8.8 %reshape.670 = bf16[640,4096]{1,0:T(8,128)(2,1)} reshape(bf16[128,5,4096]{2,1,0:T(8,128)(2,1)} %all-gather.13.cloned.1.call-done) | data formatting | bytes 10485760
  225.8 4.3 fusion.46
  237.2 45.6 %all-gather.9.cloned.1.call-done = bf16[2048,640]{1,0:T(8,128)(2,1)} async-done(((bf16[16,640]{1,0:T(8,128)(2,1)}), bf16[2048,640]{1,0:T(8,128)(2,1)}) %all-gather.9.cloned.1.call-update) | async-done | bytes 2621456 | tf_op jit(solution)/shard_map/all_gather | solution.py:205
  298.0 11.0 %fusion.23 = (bf16[256,2048]{1,0:T(8,128)(2,1)S(1)}, bf16[256,2048]{1,0:T(8,128)(2,1)S(1)}) fusion(f32[256,2048]{1,0:T(8,128)S(1)} %copy-done.49, f32[256,2048]{1,0:T(8,128)S(1)} %copy-done.129, bf16[256,640]{1,0:T(8,128)(2,1)S(1)} %get-tuple-element.95, bf16[2048,640]{1,0:T(8,128)(2,1)S(1)} %copy-done.128), kind=kOutput, calls=%fused_computation.42 | convolution fusion | flops 683671552 | bytes 9240576 | tf_op jit(solution)/shard_map/td,fd->tf/dot_general | solution.py:228
  317.0 3.9 fusion.58
  352.8 4.3 all-to-all-start
  360.0 6.1 convolution_add_fusion.2
  375.5 6.3 reshape_reshape.9
  381.8 6.3 reshape_reshape.10
  388.2 5.5 reshape_reshape.11
  393.7 17.0 %concatenate.45 = f32[128,30730]{1,0:T(8,128)} concatenate(f32[128,10240]{1,0:T(8,128)} %reshape_reshape.9, f32[128,10240]{1,0:T(8,128)} %reshape_reshape.10, f32[128,10240]{1,0:T(8,128)} %reshape_reshape.11, f32[128,5]{1,0:T(8,128)S(1)} %add.370, f32[128,5]{1,0:T(8,128)S(1)} %add.372), dimensions={1} | concatenate | bytes 31467520 | tf_op jit(solution)/shard_map/concatenate | solution.py:48
  410.6 11.0 %pad.36 = f32[128,31744]{1,0:T(8,128)} pad(f32[128,30730]{1,0:T(8,128)} %concatenate.45, f32[]{:T(128)} %constant.58.clone.1), padding=0_0x0_1014 | pad | bytes 31986692 | tf_op jit(solution)/shard_map/jit(_pad)/pad | solution.py:50
  421.6 14.0 %reshape.646 = f32[31744,128]{1,0:T(8,128)} reshape(f32[128,31744]{1,0:T(8,128)} %pad.36) | data formatting | bytes 32505856 | tf_op jit(solution)/shard_map/reshape | solution.py:50
  438.8 4.2 all-to-all-start.1
  448.5 9.1 %all-to-all-done.1 = bf16[4,256,512]{1,2,0:T(8,128)(2,1)} async-done(((bf16[4,256,512]{1,2,0:T(8,128)(2,1)}), bf16[4,256,512]{1,2,0:T(8,128)(2,1)}, u32[]{:S(2)}, u32[]{:S(2)}) %all-to-all-start.1) | async-done | bytes 1048608 | tf_op jit(solution)/shard_map/all_to_all | solution.py:34
  471.4 64.5 %all-reduce.24 = (f32[640]{0:T(1024)S(1)}, f32[640]{0:T(1024)S(1)}, f32[256]{0:T(256)S(1)}, f32[256]{0:T(256)S(1)}) all-reduce(f32[640]{0:T(1024)S(1)} %add.362, f32[640]{0:T(1024)S(1)} %add.363, f32[256]{0:T(256)S(1)} %add.364, f32[256]{0:T(256)S(1)} %add.365), channel_id=6, replica_groups=mesh['fsdp'=32,'dp'=4] {'fsdp','dp'}, use_global_device_ids=true, to_apply=%region_44.45.clone | all-reduce | flops 1792 | bytes 14336
  541.3 150.6 %all-reduce.29.cloned.1.call-done = (f32[640,1024]{1,0:T(8,128)}, f32[640,256]{1,0:T(8,128)}, f32[640,256]{1,0:T(8,128)}, f32[1024,640]{1,0:T(8,128)}, f32[31744,128]{1,0:T(8,128)}) async-done(((f32[640,1024]{1,0:T(8,128)}, f32[640,256]{1,0:T(8,128)}, f32[640,256]{1,0:T(8,128)}, f32[1024,640]{1,0:T(8,128)}, f32[31744,128]{1,0:T(8,128)}), (f32[640,1024]{1,0:T(8,128)}, f32[640,256]{1,0:T(8,128)}, ...) | async-done | bytes 22806544
  (456 shorter events, 147.6 us)
Async XLA Ops:
  7.2 83.9 %all-gather.11.cloned.1.call-start = ((), (), s32[]{:S(2)}) async-start(), calls=%async_computation.4 | async-start | bytes 3170304 | tf_op jit(solution)/shard_map/all_gather | solution.py:23
  8.6 136.7 %all-gather.7.cloned.1.call-start = ((), (), s32[]{:S(2)}) async-start(), calls=%async_computation.2 | async-start | bytes 1320960 | tf_op jit(solution)/shard_map/all_gather | solution.py:139
  9.4 207.6 %all-gather.13.cloned.1.call-start = ((), (), s32[]{:S(2)}) async-start(), calls=%async_computation.5 | async-start | bytes 8454144 | tf_op jit(solution)/shard_map/all_gather | solution.py:23
  10.9 271.9 %all-gather.9.cloned.1.call-start = ((), (), s32[]{:S(2)}) async-start(), calls=%async_computation.3 | async-start | bytes 2641920 | tf_op jit(solution)/shard_map/all_gather | solution.py:205
  11.5 110.5 %copy-start.126 = (f32[128]{0:T(128)}, f32[128]{0:T(128)S(1)}, u32[]{:S(2)}) copy-start(f32[128]{0:T(128)S(1)} %multiply_exponential_fusion) | copy-start | bytes 1540
  86.2 35.7 %copy-start.110 = (f32[256]{0:T(256)}, f32[256]{0:T(256)S(1)}, u32[]{:S(2)}) copy-start(f32[256]{0:T(256)S(1)} %convert_element_type.246) | copy-start | bytes 3076
  86.2 48.1 %copy-start.116 = (f32[256]{0:T(256)}, f32[256]{0:T(256)S(1)}, u32[]{:S(2)}) copy-start(f32[256]{0:T(256)S(1)} %convert_element_type.251) | copy-start | bytes 3076
  89.3 32.7 %copy-start.112 = (f32[256]{0:T(256)}, f32[256]{0:T(256)S(1)}, u32[]{:S(2)}) copy-start(f32[256]{0:T(256)S(1)} %dynamic-slice_convert_fusion.1) | copy-start | bytes 3076
  89.6 32.4 %copy-start.114 = (f32[256]{0:T(256)}, f32[256]{0:T(256)S(1)}, u32[]{:S(2)}) copy-start(f32[256]{0:T(256)S(1)} %dynamic-slice_convert_fusion) | copy-start | bytes 3076
  94.9 27.0 %copy-start.38 = (f32[256,256]{0,1:T(8,128)}, f32[256,256]{0,1:T(8,128)S(1)}, u32[]{:S(2)}) copy-start(f32[256,256]{0,1:T(8,128)S(1)} %get-tuple-element.147) | copy-start | bytes 786436
  99.3 34.9 %copy-start.96 = (f32[256,4]{0,1:T(4,128)}, f32[256,4]{0,1:T(4,128)S(1)}, u32[]{:S(2)}) copy-start(f32[256,4]{0,1:T(4,128)S(1)} %get-tuple-element.150) | copy-start | bytes 12292
  99.4 34.9 %copy-start.14 = (f32[256,4,256]{0,2,1:T(8,128)}, f32[256,4,256]{0,2,1:T(8,128)S(1)}, u32[]{:S(2)}) copy-start(f32[256,4,256]{0,2,1:T(8,128)S(1)} %get-tuple-element.151) | copy-start | bytes 3145732
  100.1 34.1 %copy-start.98 = (f32[256,4]{0,1:T(4,128)}, f32[256,4]{0,1:T(4,128)S(1)}, u32[]{:S(2)}) copy-start(f32[256,4]{0,1:T(4,128)S(1)} %get-tuple-element.148) | copy-start | bytes 12292
  100.1 34.2 %copy-start.16 = (f32[256,4,256]{0,2,1:T(8,128)}, f32[256,4,256]{0,2,1:T(8,128)S(1)}, u32[]{:S(2)}) copy-start(f32[256,4,256]{0,2,1:T(8,128)S(1)} %get-tuple-element.149) | copy-start | bytes 3145732
  100.1 34.1 %copy-start.100 = (f32[256]{0:T(256)}, f32[256]{0:T(256)S(1)}, u32[]{:S(2)}) copy-start(f32[256]{0:T(256)S(1)} %fusion.200) | copy-start | bytes 3076
  100.2 34.0 %copy-start.102 = (f32[256]{0:T(256)}, f32[256]{0:T(256)S(1)}, u32[]{:S(2)}) copy-start(f32[256]{0:T(256)S(1)} %fusion.195) | copy-start | bytes 3076
  123.2 35.7 %copy-start.63 = (f32[256,128]{0,1:T(8,128)}, f32[256,128]{0,1:T(8,128)S(1)}, u32[]{:S(2)}) copy-start(f32[256,128]{0,1:T(8,128)S(1)} %get-tuple-element.115) | copy-start | bytes 393220
  352.8 86.0 %all-to-all-start = ((bf16[4,256,512]{1,2,0:T(8,128)(2,1)}), bf16[4,256,512]{1,2,0:T(8,128)(2,1)}, u32[]{:S(2)}, u32[]{:S(2)}) async-start(bf16[4,256,512]{1,2,0:T(8,128)(2,1)} %bitcast.293), calls=%async_computation | async-start | bytes 2097152 | tf_op jit(solution)/shard_map/all_to_all | solution.py:34
  374.3 61.2 %copy-start.46 = (bf16[256,4,256]{0,2,1:T(8,128)(2,1)}, bf16[256,4,256]{0,2,1:T(8,128)(2,1)S(1)}, u32[]{:S(2)}) copy-start(bf16[256,4,256]{0,2,1:T(8,128)(2,1)S(1)} %get-tuple-element.120) | copy-start | bytes 1572868
  438.8 18.7 %all-to-all-start.1 = ((bf16[4,256,512]{1,2,0:T(8,128)(2,1)}), bf16[4,256,512]{1,2,0:T(8,128)(2,1)}, u32[]{:S(2)}, u32[]{:S(2)}) async-start(bf16[4,256,512]{1,2,0:T(8,128)(2,1)} %bitcast.294), calls=%async_computation.1 | async-start | bytes 2097152 | tf_op jit(solution)/shard_map/all_to_all | solution.py:34
  443.1 248.8 %all-reduce.29.cloned.1.call-start = ((), (), s32[]{:S(2)}) async-start(), calls=%async_computation.6 | async-start | bytes 45613056
  469.8 68.5 %copy-start.107 = (f32[256]{0:T(256)S(1)}, f32[256]{0:T(256)}, u32[]{:S(2)}) copy-start(f32[256]{0:T(256)} %copy-done.106) | copy-start | bytes 3076
  469.8 68.5 %copy-start.109 = (f32[256]{0:T(256)S(1)}, f32[256]{0:T(256)}, u32[]{:S(2)}) copy-start(f32[256]{0:T(256)} %copy-done.108) | copy-start | bytes 3076
  469.8 68.5 %copy-start.22 = (f32[256,640]{1,0:T(8,128)S(1)}, f32[256,640]{1,0:T(8,128)}, u32[]{:S(2)}) copy-start(f32[256,640]{1,0:T(8,128)} %copy-done.21) | copy-start | bytes 1966084
  (119 other events, 553.7 us)
Sparse Core Ops, SparseCore 0:
  11.7 69.4 all-gather.10
  84.0 61.3 all-gather.6
  149.1 67.8 all-gather.12
  219.8 62.9 all-gather.8
  463.7 228.0 all-reduce.28
where the time goes:
time: 718 us; the launch traced here: 707 us
  waiting for transfers between devices  264 us (37%)
  blocking collectives  178 us (25%)
  local copies, waits for them, and re-layouts  109 us (15%)
  matrix products  99.1 us (14%)
  other arithmetic  32.1 us (4%)
  between operations  16.2 us (2%)
  starting transfers between devices  8.95 us (1%)
    unnamed x6, waiting for transfers between devices  152 us
    unnamed x2, blocking collectives  134 us
    all_gather x2, waiting for transfers between devices, side_by_side(): lax.all_gather(both, axis, axis=dim, tiled=True)  51 us
    all_gather x1, waiting for transfers between devices, on_device(): lax.all_gather(w_down, ('fsdp', 'dp'), axis=0, tiled=True)  45.6 us
    unnamed x293, local copies, waits for them, and re-layouts  36.7 us
    all_gather x2, blocking collectives, on_device(): lax.all_gather(keys_own, 'dp', axis=0, tiled=True)  22.4 us
    all_gather x2, blocking collectives, on_device(): lax.all_gather(values_own, 'dp', axis=0, tiled=True)  21.7 us
    another operation x3, local copies, waits for them, and re-layouts, one_scatter(): lines = jnp.concatenate([b.reshape(peers, -1) for b in blocks], axis=1)  18.2 us
  transfers between devices with their start and end apart: 7, of which 5 were waited for; matrix products, arithmetic and copies ran while one was open for 21% of the time, Pallas kernels for 0%

commit v1 on v0

v1 whole, which is shorter than its diff:
```python
import math

import jax
import jax.numpy as jnp
from jax import lax
from jax.experimental import pallas as pl
from jax.experimental.pallas import tpu as pltpu
from jax.sharding import PartitionSpec as P

MESH = pl.DeviceIdType.MESH
F32 = jnp.float32
BF = jnp.bfloat16
I32 = jnp.int32
EPS = 1e-06
THETA = 1000000.0
T = 512
D = 640
GAINS = ((0, 5, 640), (5, 5, 640), (10, 2, 256), (12, 2, 256), (14, 5, 640), (19, 5, 640))
N_SEM = 224


def mm(a, b):
    return lax.dot_general(a, b, (((1,), (0,)), ((), ())), preferred_element_type=F32)


def mm_nt(a, b):
    return lax.dot_general(a, b, (((1,), (1,)), ((), ())), preferred_element_type=F32)


def mm_tn(a, b):
    return lax.dot_general(a, b, (((0,), (0,)), ((), ())), preferred_element_type=F32)


def mean_last(v):
    return jnp.mean(v, -1, keepdims=True)


def inv_rms(v):
    return lax.rsqrt(mean_last(v * v) + EPS)


def iota(shape, dim):
    return lax.broadcasted_iota(I32, shape, dim)


def norm_back(v, gain, grad):
    r = inv_rms(v)
    hat = v * r
    gg = grad * gain
    return r * (gg - hat * mean_last(gg * hat)), grad * hat


def kernel(
    tok, cot, dl, gains, wq, wk, wv, wo, wg, wu, wd,
    o_layer, o_gx, o_q, o_k, o_v, o_o, o_gate, o_up, o_down, o_g0, o_g1, o_g2, o_g3, o_g4, o_g5,
    W1, W2, W3, W4, W5, GW, stf, stage, R1, mf, po, PR, DLB,
    XB, CB, NRM, CS, SN, DCOL, DROW, GV, QR, Q, KR, KV, AM, LI, OA, LA, BR, HID, NF, GT, UT, HM, ACC, GD, LO,
    DAM, DD, DKV, DKR, GXR,
    G2, G3, G4, G5, C1, C2, C3, C4, C5, A1, A2, A3, A4, A5, B1, B2, B3, B4, B5, E1, E2, E3, E4, E5,
    GG, GGR, F2, R2, c4f, R4, ss, rs, ls,
):
    f = lax.axis_index("fsdp")
    y = lax.axis_index("dp")
    x = f // 8
    z = (f // 2) % 4
    c = f % 2
    zh, zl = z // 2, z % 2
    me = {"x": x, "z": z, "c": c, "y": y}
    gi = c * 8 + zl * 4 + y
    ge = zl * 8 + c * 4 + y

    def dev(co):
        return ((co["x"] * 4 + co["z"]) * 2 + co["c"], co["y"])

    def member(j):
        return {"x": x, "z": zh * 2 + (j // 4) % 2, "c": j // 8, "y": j % 4}

    def moved(axis, k):
        co = dict(me)
        co[axis] = (me[axis] + k) % (2 if axis == "c" else 4)
        return co

    count = [0]

    def fresh():
        count[0] += 1
        assert count[0] <= N_SEM
        return count[0] - 1

    sent = []

    def send(src, dst, co):
        i = fresh()
        cp = pltpu.make_async_remote_copy(
            src_ref=src, dst_ref=dst, send_sem=ss.at[i], recv_sem=rs.at[i], device_id=dev(co), device_id_type=MESH
        )
        cp.start()
        sent.append(cp)
        return cp

    def arrived(cps):
        for cp in cps:
            cp.wait_recv()

    def sl_cols(r0, rn):
        def sl(co, done):
            xs = slice(None) if "x" in done else pl.ds(co["x"], 1)
            zs = slice(None) if "z" in done else pl.ds(co["z"] // 2, 1)
            if "y" not in done:
                cs, w = co["c"] * 1024 + (co["z"] % 2) * 512 + co["y"] * 128, 128
            elif "z" not in done:
                cs, w = co["c"] * 1024 + (co["z"] % 2) * 512, 512
            else:
                cs, w = co["c"] * 1024, 1024
            return (xs, zs, pl.ds(r0, rn), pl.ds(pl.multiple_of(cs, 128), w))
        return sl

    def sl_out(co, done):
        xs = slice(None) if "x" in done else pl.ds(co["x"], 1)
        zs = slice(None) if "z" in done else pl.ds(co["z"], 1)
        if "y" in done:
            return (xs, zs, pl.ds(co["c"], 1), pl.ds(0, 32), pl.ds(0, 768))
        return (
            xs, zs, pl.ds(co["c"], 1),
            pl.ds(pl.multiple_of((co["y"] // 2) * 16, 16), 16), pl.ds(pl.multiple_of((co["y"] % 2) * 384, 128), 384),
        )

    def sl_down(co, done):
        xs = slice(None) if "x" in done else pl.ds(co["x"], 1)
        zs = slice(None) if "z" in done else pl.ds(co["z"], 1)
        rows = pl.ds(0, 64) if "y" in done else pl.ds(pl.multiple_of(co["y"] * 16, 16), 16)
        return (xs, zs, pl.ds(co["c"], 1), rows, pl.ds(0, 640))

    pieces = {
        "1a": (W1, sl_cols(0, 48), "yzx"),
        "1b": (W1, sl_cols(48, 32), "yxz"),
        "2": (W2, sl_cols(0, 80), "yzx"),
        "3": (W3, sl_cols(0, 80), "yxz"),
        "4": (W4, sl_out, "yzx"),
        "5": (W5, sl_down, "zxy"),
    }

    def gather(name, phase):
        w, sl, order = pieces[name]
        ref = w.at[sl(me, order[:phase])]
        if phase == 3:
            return [send(ref, ref, moved("c", 1))]
        return [send(ref, ref, moved(order[phase], k)) for k in (1, 2, 3)]

    bar = pltpu.get_barrier_semaphore()
    friends = [member((gi + d) % 16) for d in range(1, 16)]
    friends += [moved("z", 2)] + [dict(me, z=(zh * 2 + 2) % 4 + (1 - zl))] + [moved("x", k) for k in (1, 2, 3)]
    for co in friends:
        pl.semaphore_signal(bar, inc=1, device_id=dev(co), device_id_type=MESH)

    grow = gains[...].astype(F32)
    for j in range(16):
        cols = slice(128 * j, 128 * j + 128)
        if j < 8:
            part = wq[:, cols]
        elif j < 10:
            part = wk[:, 128 * (j - 8):128 * (j - 7)]
        elif j < 12:
            part = wv[:, 128 * (j - 10):128 * (j - 9)]
        else:
            part = None
        stf[j, 0:5, :] = jnp.zeros((5, 128), F32) if part is None else part.astype(F32)
        stf[j, 5:10, :] = wg[:, cols].astype(F32)
        stf[j, 10:15, :] = wu[:, cols].astype(F32)
        stf[j, 15:16, :] = grow
    stage[...] = stf[...].astype(BF)
    wof = wo[...].astype(F32)
    twice = jnp.concatenate([wof, wof], axis=0)
    keep = (iota((16, 640), 0) // 8) == (y % 2)
    twice = jnp.where(keep, twice, 0.0).astype(BF)
    po[0, :, :] = twice[:, 0:384]
    po[1, :, 0:256] = twice[:, 384:640]
    po[1, :, 256:384] = jnp.zeros((16, 128), BF)
    rowid = iota((8, 128), 0)
    tile = jnp.zeros((8, 128), I32)
    for m in range(2):
        for k in range(3):
            tile = jnp.where(rowid == 3 * m + k, dl[0, m, k], tile)
    DLB[c] = tile
    W5[x, z, c, pl.ds(pl.multiple_of(y * 16, 16), 16), :] = wd[...]

    pl.semaphore_wait(bar, len(friends))

    core_to = ((y + 1) // 2) % 2
    blocks = (c, 3 - c)

    def reshard(src, dst):
        s_base, r_base = fresh(), fresh()
        s2, r2 = fresh(), fresh()
        ops = []
        for m, si in ((0, s_base), (1, s2)):
            to = dict(me, c=core_to, y=c + 2 * m)
            own = jnp.logical_and(to["c"] == c, to["y"] == y)
            slot = y // 2

            def far(r, m=m, si=si, to=to):
                return pltpu.make_async_remote_copy(
                    src_ref=src.at[m], dst_ref=dst.at[0 if r == r_base else 1], send_sem=ss.at[si],
                    recv_sem=rs.at[r], device_id=dev(to), device_id_type=MESH,
                )

            for sv, r in ((0, r_base), (1, r2)):
                @pl.when(jnp.logical_and(jnp.logical_not(own), slot == sv))
                def _(far=far, r=r):
                    far(r).start()

                @pl.when(jnp.logical_and(own, slot == sv))
                def _(m=m, sv=sv):
                    cp = pltpu.make_async_copy(src.at[m], dst.at[sv], ls)
                    cp.start()
                    cp.wait()

            ops.append((own, far(r_base)))

        def wait_in():
            for s, r in ((0, r_base), (1, r2)):
                mine = jnp.logical_and(blocks[s] == y, c == y % 2)

                @pl.when(jnp.logical_not(mine))
                def _(s=s, r=r):
                    pltpu.make_async_remote_copy(
                        src_ref=src.at[0], dst_ref=dst.at[s], send_sem=ss.at[s_base], recv_sem=rs.at[r],
                        device_id=dev(moved("c", 1)), device_id_type=MESH,
                    ).wait_recv()

        def wait_out():
            for own, cp in ops:
                @pl.when(jnp.logical_not(own))
                def _(cp=cp):
                    cp.wait_send()

        return wait_in, wait_out

    def unshard(src, dst):
        r0, r1 = fresh(), fresh()
        ops = []
        m = y // 2
        for s, si in ((0, r0), (1, r1)):
            to = dict(me, c=y % 2, y=blocks[s])
            own = jnp.logical_and(to["c"] == c, to["y"] == y)

            def far(mv, r, s=s, si=si, to=to):
                return pltpu.make_async_remote_copy(
                    src_ref=src.at[s], dst_ref=dst.at[mv], send_sem=ss.at[si], recv_sem=rs.at[r],
                    device_id=dev(to), device_id_type=MESH,
                )

            for mv, r in ((0, r0), (1, r1)):
                @pl.when(jnp.logical_and(jnp.logical_not(own), m == mv))
                def _(far=far, mv=mv, r=r):
                    far(mv, r).start()

                @pl.when(jnp.logical_and(own, m == mv))
                def _(s=s, mv=mv):
                    cp = pltpu.make_async_copy(src.at[s], dst.at[mv], ls)
                    cp.start()
                    cp.wait()

            ops.append((own, far(0, r0)))

        def wait_in():
            for mv, r in ((0, r0), (1, r1)):
                mine = jnp.logical_and(core_to == c, y == c + 2 * mv)

                @pl.when(jnp.logical_not(mine))
                def _(mv=mv, r=r):
                    pltpu.make_async_remote_copy(
                        src_ref=src.at[0], dst_ref=dst.at[mv], send_sem=ss.at[r0], recv_sem=rs.at[r],
                        device_id=dev(moved("c", 1)), device_id_type=MESH,
                    ).wait_recv()

        def wait_out():
            for own, cp in ops:
                @pl.when(jnp.logical_not(own))
                def _(cp=cp):
                    cp.wait_send()

        return wait_in, wait_out

    a2a = []
    for d in range(1, 16):
        j = (gi + d) % 16
        a2a.append(send(stage.at[j], R1.at[ge], member(j)))
    R1[ge] = stage[gi]
    pair = [send(po.at[1 - y % 2], PR, dict(me, y=y + 1 - 2 * (y % 2)))]
    lens_cp = [send(DLB.at[c], DLB.at[c], moved("c", 1))]
    x_in, x_out = reshard(tok, XB)

    arrived(a2a)
    for e in range(16):
        v = R1[e].astype(F32)
        for k in range(3):
            mf[k, 5 * e:5 * e + 5, :] = v[5 * k:5 * k + 5, :]
        mf[3, e:e + 1, :] = v[15:16, :]
    own_cols = pl.ds(pl.multiple_of(c * 1024 + zl * 512 + y * 128, 128), 128)
    for w, k in ((W1, 0), (W2, 1), (W3, 2)):
        w[x, zh, :, own_cols] = mf[k].astype(BF)
    GW[x, zh] = mf[3, 0:16, :].astype(BF)
    g1a, g1b = gather("1a", 0), gather("1b", 0)
    gz = [send(GW.at[x, zh], GW.at[x, zh], moved("z", 2))]
    arrived(pair)
    W4[x, z, c, pl.ds(pl.multiple_of((y // 2) * 16, 16), 16), pl.ds(pl.multiple_of((y % 2) * 384, 128), 384)] = (
        po[y % 2].astype(F32) + PR[...].astype(F32)
    ).astype(BF)

    arrived(lens_cp)
    lt = DLB[y % 2]
    first = y // 2 == 0
    l0 = jnp.where(first, lt[0:1, :], lt[3:4, :])[:, 0:1]
    l1 = jnp.where(first, lt[1:2, :], lt[4:5, :])[:, 0:1]
    e0, e1 = l0, l0 + l1
    freq = jnp.exp(iota((1, 128), 1).astype(F32) * (-2.0 * math.log(THETA) / 256))
    for s in range(2):
        t = blocks[s] * 256 + iota((256, 1), 0)
        p0, p1 = (t >= e0).astype(I32), (t >= e1).astype(I32)
        DCOL[s] = p0 + p1
        turned = (t - p0 * l0 - p1 * l1).astype(F32) * freq
        CS[s] = jnp.cos(turned)
        SN[s] = jnp.sin(turned)
    for k in range(4):
        t = 256 * k + iota((1, 256), 1)
        DROW[k] = (t >= e0).astype(I32) + (t >= e1).astype(I32)

    arrived(g1a + g1b)
    g1a, g1b = gather("1a", 1), gather("1b", 1)
    arrived(gz)
    gx = [send(GW.at[x], GW.at[x], moved("x", k)) for k in (1, 2, 3)]
    g2, g3, g4, g5 = gather("2", 0), gather("3", 0), gather("4", 0), gather("5", 0)
    x_in()
    arrived(g1a + g1b)
    g1a, g1b = gather("1a", 2), gather("1b", 2)
    arrived(gx)

    packed = GW[...].reshape(128, 128)
    for k, (lane, per, width) in enumerate(GAINS):
        col = iota((128, width), 1)
        shard = iota((128, width), 0)
        colf = col.astype(F32)
        rest = colf - per * jnp.floor((colf + 0.5) * (1.0 / per))
        pick = jnp.where(shard.astype(F32) == rest + lane, 1.0, 0.0).astype(BF)
        spread = mm(packed, pick)
        mine = jnp.logical_and(col >= per * shard, col < per * shard + per)
        GV[k:k + 1, 0:width] = jnp.sum(jnp.where(mine, spread, 0.0), 0, keepdims=True)

    def rows(n, fn):
        def step(i, carry):
            fn(pl.ds(pl.multiple_of(i * n, n), n))
            return carry
        lax.fori_loop(0, T // n, step, 0)

    xv = XB.reshape(T, D)
    cv = CB.reshape(T, D)
    csv, snv = CS.reshape(T, 128), SN.reshape(T, 128)

    def do_norm(r):
        v = xv[r, :].astype(F32)
        NRM[r, :] = (v * inv_rms(v) * GV[0:1, :]).astype(BF)
    rows(128, do_norm)
    arrived(g1a + g1b)
    g1a, g1b = gather("1a", 3), gather("1b", 3)
    arrived(g2 + g3 + g4 + g5)
    g4, g2, g3, g5 = gather("4", 1), gather("2", 1), gather("3", 1), gather("5", 1)
    arrived(g1a + g1b)

    def w1_cols(start, width):
        return W1[:, :, :, pl.ds(pl.multiple_of(start, 128), width)].reshape(D, width)

    def turn(u, cs, sn):
        u1, u2 = u[:, 0:128], u[:, 128:256]
        return u1 * cs - u2 * sn, u2 * cs + u1 * sn

    def turn_back(u, cs, sn):
        u1, u2 = u[:, 0:128], u[:, 128:256]
        return jnp.concatenate([u1 * cs + u2 * sn, u2 * cs - u1 * sn], -1)

    raw = mm(NRM[...], w1_cols(1024, 256))
    KR[...] = raw
    o1, o2 = turn(raw * inv_rms(raw) * GV[3:4, 0:256], csv[...], snv[...])
    vals = mm(NRM[...], w1_cols(1280, 256))
    for s in range(2):
        r = slice(256 * s, 256 * s + 256)
        KV[blocks[s], :, 0:128] = o1[r].astype(BF)
        KV[blocks[s], :, 128:256] = o2[r].astype(BF)
        KV[blocks[s], :, 256:512] = vals[r].astype(BF)
    kv_cp = [send(KV.at[blocks[s]], KV.at[blocks[s]], moved("c", 1)) for s in range(2)]

    def do_query(h, carry):
        raw = mm(NRM[...], w1_cols(h * 256, 256))
        QR[h] = raw.astype(BF)
        o1, o2 = turn(raw * inv_rms(raw) * GV[2:3, 0:256], csv[...], snv[...])
        for s in range(2):
            r = slice(256 * s, 256 * s + 256)
            Q[s, h, :, 0:128] = (o1[r] * 0.0625).astype(BF)
            Q[s, h, :, 128:256] = (o2[r] * 0.0625).astype(BF)
        return carry
    lax.fori_loop(0, 4, do_query, 0)

    arrived(g2 + g3 + g4 + g5)
    g4, g2, g3, g5 = gather("4", 2), gather("2", 2), gather("3", 2), gather("5", 2)
    c_in, c_out = reshard(cot, CB)
    arrived(kv_cp)

    def seen(s, kb):
        t = blocks[s] * 256 + iota((256, 256), 0)
        k = kb * 256 + iota((256, 256), 1)
        return jnp.logical_and(DCOL[s] == DROW[kb], t >= k)

    for s in range(2):
        OA[...] = jnp.zeros_like(OA)
        LA[...] = jnp.zeros_like(LA)

        def forward(kb, carry, s=s):
            vis = seen(s, kb)
            keys, vals = KV[kb, :, 0:256], KV[kb, :, 256:512]
            for h in range(4):
                p = jnp.where(vis, jnp.exp(mm_nt(Q[s, h], keys)), 0.0)
                LA[h] += jnp.sum(p, -1, keepdims=True)
                OA[h] += mm(p.astype(BF), vals)
            return carry
        lax.fori_loop(0, blocks[s] + 1, forward, 0)
        for h in range(4):
            inv = 1.0 / LA[h]
            LI[s, h] = inv
            AM[256 * s:256 * s + 256, 256 * h:256 * h + 256] = (OA[h] * inv).astype(BF)
        if s == 0:
            arrived(g4)
            g4 = gather("4", 3)
    arrived(g4)
    w4v = W4.reshape(1024, 768)
    w5v = W5.reshape(2048, 640)

    def do_out(r):
        b = mm(AM[r, :], w4v[:, 0:640])
        BR[r, :] = b
        hid = xv[r, :].astype(F32) + b * inv_rms(b) * GV[1:2, :]
        HID[r, :] = hid
        NF[r, :] = (hid * inv_rms(hid) * GV[4:5, :]).astype(BF)
    rows(256, do_out)
    arrived(g2 + g3 + g5)
    g2, g3, g5 = gather("2", 3), gather("3", 3), gather("5", 3)
    arrived(g2 + g3 + g5)

    def cols_of(w, at, width):
        return w[:, :, :, pl.ds(pl.multiple_of(at, 128), width)].reshape(D, width)

    def do_ffn(n, carry):
        at = pl.ds(pl.multiple_of(n * 256, 256), 256)
        gate = mm(NF[...], cols_of(W2, n * 256, 256))
        up = mm(NF[...], cols_of(W3, n * 256, 256))
        GT[:, at] = gate.astype(BF)
        UT[:, at] = up.astype(BF)
        HM[:, at] = (jax.nn.gelu(gate, approximate=True) * up).astype(BF)
        return carry
    lax.fori_loop(0, 8, do_ffn, 0)

    c_in()
    GG[...] = jnp.zeros_like(GG)
    lov = LO.reshape(T, D)

    def do_down(r):
        d = mm(HM[r, :], w5v[...])
        rd = inv_rms(d)
        hat = d * rd
        lov[r, :] = (HID[r, :] + hat * GV[5:6, :]).astype(BF)
        g = cv[r, :].astype(F32)
        gg = g * GV[5:6, :]
        GD[r, :] = (rd * (gg - hat * mean_last(gg * hat))).astype(BF)
        GG[5:6, :] += jnp.sum(g * hat, 0, keepdims=True)
    rows(256, do_down)
    lo_in, lo_out = unshard(LO, o_layer)

    g5v = G5.reshape(2048, 640)
    ACC[...] = jnp.zeros_like(ACC)

    def do_ffn_back(n, carry):
        at = pl.ds(pl.multiple_of(n * 256, 256), 256)
        g5v[at, :] = mm_tn(HM[:, at], GD[...]).astype(BF)
        dh = mm_nt(GD[...], w5v[at, :])
        gate, up = GT[:, at].astype(F32), UT[:, at].astype(F32)
        k0, k1 = math.sqrt(2.0 / math.pi), 0.044715
        th = jnp.tanh(k0 * (gate + k1 * gate * gate * gate))
        half = 0.5 * (1.0 + th)
        slope = half + 0.5 * gate * (1.0 - th * th) * k0 * (1.0 + 3.0 * k1 * gate * gate)
        dg = (dh * up * slope).astype(BF)
        du = (dh * (gate * half)).astype(BF)
        nf = NF[...]
        G2[:, :, :, at] = mm_tn(nf, dg).astype(BF).reshape(4, 2, 80, 256)
        G3[:, :, :, at] = mm_tn(nf, du).astype(BF).reshape(4, 2, 80, 256)
        ACC[...] += mm_nt(dg, cols_of(W2, n * 256, 256)) + mm_nt(du, cols_of(W3, n * 256, 256))
        return carry
    lax.fori_loop(0, 8, do_ffn_back, 0)

    red = {
        "2": (G2, sl_cols(0, 80), "yzx", C2, (A2, B2, E2)),
        "3": (G3, sl_cols(0, 80), "yxz", C3, (A3, B3, E3)),
        "4": (G4, sl_out, "yzx", C4, (A4, B4, E4)),
        "5": (G5, sl_down, "zxy", C5, (A5, B5, E5)),
        "1": (W2, sl_cols(0, 80), "yzx", C1, (A1, B1, E1)),
    }

    def sum_core(name):
        g, sl, order, cbuf, _ = red[name]
        return [send(g.at[sl(moved("c", 1), order)], cbuf, moved("c", 1))]

    def leading(shape):
        return shape[0] * shape[1]

    def part(ref_idx, i, shape):
        n1 = shape[1]
        def one(s, k):
            base = 0 if s == slice(None) else s.start
            return pl.ds(base + k, 1)
        return (one(ref_idx[0], i // n1), one(ref_idx[1], i % n1)) + tuple(ref_idx[2:])

    def add_in(name, idx, bufs, out=None):
        g = red[name][0]
        shape = bufs[0].shape

        def step(i, carry):
            at = part(idx, i, shape)
            bat = (pl.ds(i // shape[1], 1), pl.ds(i % shape[1], 1))
            tot = g[at].astype(F32)
            for b in bufs:
                tot = tot + b[bat].astype(F32)
            if out is None:
                g[at] = tot.astype(BF)
            else:
                out(tot)
            return carry
        if leading(shape) == 1:
            step(0, 0)
        else:
            lax.fori_loop(0, leading(shape), step, 0)

    def add_core(name, cps):
        arrived(cps)
        g, sl, order, cbuf, _ = red[name]
        add_in(name, sl(me, order), [cbuf])

    def sum_phase(name, phase):
        g, sl, order, _, bufs = red[name]
        axis, done = order[2 - phase], order[:2 - phase]
        out = []
        for k in (1, 2, 3):
            co = moved(axis, k)
            out.append(send(g.at[sl(co, done)], bufs[phase].at[k - 1], co))
        return out

    def add_phase(name, phase, cps, out=None):
        arrived(cps)
        g, sl, order, _, bufs = red[name]
        add_in(name, sl(me, order[:2 - phase]), [bufs[phase].at[k] for k in range(3)], out)

    s2, s3, s5 = sum_core("2"), sum_core("3"), sum_core("5")

    def do_mid(r):
        g = cv[r, :].astype(F32)
        dv, rowg = norm_back(HID[r, :], GV[4:5, :], ACC[r, :])
        GG[4:5, :] += jnp.sum(rowg, 0, keepdims=True)
        gh = g + dv
        HID[r, :] = gh
        db, rowo = norm_back(BR[r, :], GV[1:2, :], gh)
        GG[1:2, :] += jnp.sum(rowo, 0, keepdims=True)
        GD[r, :] = db.astype(BF)
    rows(128, do_mid)
    g4v = G4.reshape(1024, 768)

    def do_out_grad(n, carry):
        at = pl.ds(pl.multiple_of(n * 256, 256), 256)
        am = AM[:, at]
        g4v[at, 0:640] = mm_tn(am, GD[...]).astype(BF)
        g4v[at, 640:768] = jnp.zeros((256, 128), BF)
        dam = mm_nt(GD[...], w4v[at, 0:640]).astype(BF)
        inner = jnp.sum(dam.astype(F32) * am.astype(F32), -1, keepdims=True)
        for s in range(2):
            DAM[s, n] = dam[256 * s:256 * s + 256]
            DD[s, n] = inner[256 * s:256 * s + 256]
        return carry
    lax.fori_loop(0, 4, do_out_grad, 0)
    add_core("2", s2)
    s2 = sum_phase("2", 0)
    add_core("3", s3)
    s3 = sum_phase("3", 0)
    add_core("5", s5)
    s5 = sum_phase("5", 0)
    s4 = sum_core("4")

    DKV[...] = jnp.zeros_like(DKV)
    for s in range(2):
        OA[...] = jnp.zeros_like(OA)

        def backward(kb, carry, s=s):
            vis = seen(s, kb)
            keys, vals = KV[kb, :, 0:256], KV[kb, :, 256:512]
            dk = jnp.zeros((256, 256), F32)
            dv = jnp.zeros((256, 256), F32)
            for h in range(4):
                q, da = Q[s, h], DAM[s, h]
                p = jnp.where(vis, jnp.exp(mm_nt(q, keys)) * LI[s, h], 0.0)
                ds = (p * (mm_nt(da, vals) - DD[s, h])).astype(BF)
                OA[h] += mm(ds, keys)
                dk = dk + mm_tn(ds, q)
                dv = dv + mm_tn(p.astype(BF), da)
            DKV[kb, :, 0:256] += dk
            DKV[kb, :, 256:512] += dv
            return carry
        lax.fori_loop(0, blocks[s] + 1, backward, 0)

        def query_back(h, carry, s=s):
            dq = turn_back(OA[h] * 0.0625, CS[s], SN[s])
            raw = QR[h, 256 * s:256 * s + 256, :].astype(F32)
            dv, rowg = norm_back(raw, GV[2:3, 0:256], dq)
            GG[2:3, 0:256] += jnp.sum(rowg, 0, keepdims=True)
            GT[256 * s:256 * s + 256, pl.ds(pl.multiple_of(h * 256, 256), 256)] = dv.astype(BF)
            return carry
        lax.fori_loop(0, 4, query_back, 0)
        if s == 0:
            add_core("4", s4)
            s4 = sum_phase("4", 0)
    for s in range(2):
        HM[256 * s:256 * s + 256, 0:512] = DKV[1 - c if s == 0 else 2 + c].astype(BF)
    dk_cp = [send(HM.at[:, pl.ds(0, 512)], DKR, moved("c", 1))]
    for cp in sent:
        cp.wait_send()
    sent.clear()
    add_phase("2", 0, s2)
    s2 = sum_phase("2", 1)
    add_phase("3", 0, s3)
    s3 = sum_phase("3", 1)
    add_phase("5", 0, s5)
    s5 = sum_phase("5", 1)
    add_phase("4", 0, s4)
    s4 = sum_phase("4", 1)
    arrived(dk_cp)
    for s in range(2):
        r = slice(256 * s, 256 * s + 256)
        tot = DKV[blocks[s]] + DKR[r, :].astype(F32)
        dk = turn_back(tot[:, 0:256], CS[s], SN[s])
        dv, rowg = norm_back(KR[r, :], GV[3:4, 0:256], dk)
        GG[3:4, 0:256] += jnp.sum(rowg, 0, keepdims=True)
        GT[r, 1024:1280] = dv.astype(BF)
        GT[r, 1280:1536] = tot[:, 256:512].astype(BF)

    nrm = NRM

    def do_qkv_grad(n, carry):
        at = pl.ds(pl.multiple_of(n * 256, 256), 256)
        W2[:, :, :, at] = mm_tn(nrm[...], GT[:, at]).astype(BF).reshape(4, 2, 80, 256)
        return carry
    lax.fori_loop(0, 6, do_qkv_grad, 0)
    W2[:, :, :, 1536:2048] = jnp.zeros((4, 2, 80, 512), BF)
    s1 = sum_core("1")
    ACC[...] = jnp.zeros_like(ACC)

    def do_dnorm(n, carry):
        at = pl.ds(pl.multiple_of(n * 256, 256), 256)
        ACC[...] += mm_nt(GT[:, at], w1_cols(n * 256, 256))
        return carry
    lax.fori_loop(0, 6, do_dnorm, 0)
    lo_out()
    gxv = LO.reshape(T, D)

    def do_x(r):
        dv, rowg = norm_back(xv[r, :].astype(F32), GV[0:1, :], ACC[r, :])
        GG[0:1, :] += jnp.sum(rowg, 0, keepdims=True)
        gxv[r, :] = (HID[r, :] + dv).astype(BF)
    rows(128, do_x)
    gx_in, gx_out = unshard(LO, GXR)
    add_core("1", s1)
    s1 = sum_phase("1", 0)

    gcp = [send(GG, GGR.at[0], moved("c", 1))]
    add_phase("2", 1, s2)
    s2 = sum_phase("2", 2)
    add_phase("3", 1, s3)
    s3 = sum_phase("3", 2)
    add_phase("5", 1, s5)
    s5 = sum_phase("5", 2)
    add_phase("4", 1, s4)
    s4 = sum_phase("4", 2)
    arrived(gcp)
    base = 1
    tot = GG[...] + GGR[0]
    gcps = []
    for a, axis in enumerate("zyx"):
        GGR[10 + a] = tot
        gcps = [send(GGR.at[10 + a], GGR.at[base + k - 1], moved(axis, k)) for k in (1, 2, 3)]
        arrived(gcps)
        for k in range(3):
            tot = tot + GGR[base + k]
        base += 3
        if a == 0:
            add_phase("1", 0, s1)
            s1 = sum_phase("1", 1)
        if a == 1:
            add_phase("1", 1, s1)
            s1 = sum_phase("1", 2)
    shard = f * 4 + y
    for ref, (k, (lane, per, width)) in zip((o_g0, o_g1, o_g2, o_g3, o_g4, o_g5), enumerate(GAINS)):
        line = tot[k:k + 1, 0:width]
        col = iota((1, width), 1)
        for r in range(per):
            ref[0:1, r:r + 1] = jnp.sum(jnp.where(col == per * shard + r, line, 0.0), 1, keepdims=True)

    def into(k):
        def out(v):
            mf[k] = v.reshape(80, 128)
        return out

    def out_down(v):
        o_down[...] = v.reshape(16, 640)

    def out_4(v):
        c4f[...] = v.reshape(16, 384)

    add_phase("2", 2, s2, into(1))
    add_phase("3", 2, s3, into(2))
    add_phase("5", 2, s5, out_down)
    add_phase("4", 2, s4, out_4)
    pair = [send(c4f.at[pl.ds(pl.multiple_of(8 * (1 - y % 2), 8), 8), :], R4, dict(me, y=y + 1 - 2 * (y % 2)))]
    add_phase("1", 2, s1, into(0))
    for e in range(16):
        for k in range(3):
            F2[e, 5 * k:5 * k + 5, :] = mf[k, 5 * e:5 * e + 5, :]
    home = []
    for d in range(1, 16):
        j = (gi + d) % 16
        home.append(send(F2.at[(j // 4) % 2 * 8 + j // 8 * 4 + j % 4], R2.at[gi], member(j)))
    R2[gi] = F2[ge]
    arrived(pair)
    own = c4f[pl.ds(pl.multiple_of(8 * (y % 2), 8), 8), :]
    left = y % 2 == 0
    o_o[:, 0:384] = jnp.where(left, own, R4[...])
    o_o[:, 384:640] = jnp.where(left, R4[...], own)[:, 0:256]
    gx_in()
    for m in range(2):
        o_gx[m] = GXR[m].astype(F32)
    arrived(home)
    for j in range(16):
        cols = slice(128 * j, 128 * j + 128)
        v = R2[j]
        if j < 8:
            o_q[:, cols] = v[0:5]
        elif j < 10:
            o_k[:, 128 * (j - 8):128 * (j - 7)] = v[0:5]
        elif j < 12:
            o_v[:, 128 * (j - 10):128 * (j - 9)] = v[0:5]
        o_gate[:, cols] = v[5:10]
        o_up[:, cols] = v[10:15]
    lo_in()
    for w in (x_out, c_out, gx_out):
        w()
    for cp in sent:
        cp.wait_send()


def scratch():
    def v(*shape, dtype=F32):
        return pltpu.VMEM(shape, dtype)

    def b(*shape):
        return pltpu.VMEM(shape, BF)

    cols = (4, 2, 80, 2048)
    out = [
        b(*cols), b(*cols), b(*cols), b(4, 4, 2, 32, 768), b(4, 4, 2, 64, 640), b(4, 2, 16, 128),
        v(16, 16, 128), b(16, 16, 128), b(16, 16, 128), v(4, 80, 128), b(2, 16, 384), b(16, 384),
        v(2, 8, 128, dtype=I32),
        b(2, 256, D), b(2, 256, D), b(T, D), v(2, 256, 128), v(2, 256, 128),
        v(2, 256, 1, dtype=I32), v(4, 1, 256, dtype=I32), v(8, D),
        b(4, T, 256), b(2, 4, 256, 256), v(T, 256), b(4, 256, 512), b(T, 1024),
        v(2, 4, 256, 1), v(4, 256, 256), v(4, 256, 1),
        v(T, D), v(T, D), b(T, D), b(T, 2048), b(T, 2048), b(T, 2048), v(T, D), b(T, D),
        b(2, 256, D),
        b(2, 4, 256, 256), v(2, 4, 256, 1), v(4, 256, 512), b(T, 512),
        b(2, 256, D),
        b(*cols), b(*cols), b(4, 4, 2, 32, 768), b(4, 4, 2, 64, 640),
        b(4, 2, 80, 1024), b(4, 2, 80, 1024), b(4, 2, 80, 1024), b(4, 4, 1, 32, 768), b(4, 4, 1, 64, 640),
        b(3, 1, 2, 80, 1024), b(3, 1, 2, 80, 1024), b(3, 4, 1, 80, 512), b(3, 1, 4, 1, 32, 768), b(3, 4, 4, 1, 16, 640),
        b(3, 1, 1, 80, 512), b(3, 1, 1, 80, 512), b(3, 1, 1, 80, 512), b(3, 1, 1, 1, 32, 768), b(3, 1, 4, 1, 16, 640),
        b(3, 1, 1, 80, 128), b(3, 1, 1, 80, 128), b(3, 1, 1, 80, 128), b(3, 1, 1, 1, 16, 384), b(3, 1, 1, 1, 16, 640),
        v(8, D), v(13, 8, D), v(16, 16, 128), v(16, 16, 128), v(16, 384), v(8, 384),
        pltpu.SemaphoreType.DMA((N_SEM,)), pltpu.SemaphoreType.DMA((N_SEM,)), pltpu.SemaphoreType.DMA,
    ]
    return out


def on_device(tokens_in, cotangent, doc_lengths, w_query, w_key, w_value, w_out, gain_attn_in, gain_attn_out,
              gain_query, gain_key, w_gate, w_up, w_down, gain_ffn_in, gain_ffn_out):
    packed = jnp.concatenate([gain_attn_in, gain_attn_out, gain_query, gain_key, gain_ffn_in, gain_ffn_out])
    packed = jnp.pad(packed, (0, 128 - packed.shape[0])).reshape(1, 128)
    vm = pl.BlockSpec(memory_space=pltpu.VMEM)
    hbm = pl.BlockSpec(memory_space=pl.ANY)
    sm = pl.BlockSpec(memory_space=pltpu.SMEM)

    def s(*shape, dtype=F32):
        return jax.ShapeDtypeStruct(shape, dtype)

    outs = pl.pallas_call(
        kernel,
        out_shape=(
            s(2, 256, D, dtype=BF), s(2, 256, D), s(5, 1024), s(5, 256), s(5, 256), s(8, D), s(5, 2048), s(5, 2048),
            s(16, D), s(1, 5), s(1, 5), s(1, 2), s(1, 2), s(1, 5), s(1, 5),
        ),
        in_specs=[hbm, hbm, sm] + [vm] * 8,
        out_specs=(hbm,) + (vm,) * 14,
        scratch_shapes=scratch(),
        compiler_params=pltpu.CompilerParams(
            collective_id=0, has_side_effects=True, vmem_limit_bytes=64 * 1024 * 1024 - 65536
        ),
        name="block",
    )(tokens_in, cotangent, doc_lengths, packed, w_query, w_key, w_value, w_out, w_gate, w_up, w_down)
    (layer_out, grad_x, gq, gk, gv, go, ggate, gup, gdown, g0, g1, g2, g3, g4, g5) = outs
    return (
        layer_out, grad_x, gq, gk, gv, go, g0.reshape(-1), g1.reshape(-1), g2.reshape(-1), g3.reshape(-1),
        ggate, gup, gdown, g4.reshape(-1), g5.reshape(-1),
    )


def solution(mesh):
    both = ("fsdp", "dp")
    row, gain = P(both, None), P(both)
    tok = P(None, both, None)
    return jax.shard_map(
        on_device,
        mesh=mesh,
        in_specs=(tok, tok, P("fsdp", None, None), row, row, row, row, gain, gain, gain, gain, row, row, row, gain, gain),
        out_specs=(tok, tok, row, row, row, row, gain, gain, gain, gain, row, row, row, gain, gain),
        check_vma=False,
    )
```

time: 718 us -> 186 us (0.26); the launches traced: 707 us -> 186 us
  waiting for transfers between devices: 264 us -> 0 us
  blocking collectives: 178 us -> 0 us
  Pallas kernels: 0 us -> 170 us
  matrix products: 99.1 us -> 0 us
  local copies, waits for them, and re-layouts: 109 us -> 15.2 us
  other arithmetic: 32.1 us -> 0 us
  between operations: 16.2 us -> 0.76 us
  starting transfers between devices: 8.95 us -> 0 us
    pallas_call x0 -> x1, Pallas kernels: none -> 170 us  [on_device(): pl.pallas_call(kernel, out_shape=(s(2, 256, D, dtype=BF), s(2, 256, D), s...]
    unnamed x6 -> x0, waiting for transfers between devices: 152 us -> none
    unnamed x2 -> x0, blocking collectives: 134 us -> none
    all_gather x4 -> x0, waiting for transfers between devices: 103 us -> none  [the longest x2 51 us: side_by_side(): lax.all_gather(both, axis, axis=dim, tiled=True)]
    dot_general x54 -> x0, matrix products: 99.1 us -> none  [the longest x2 13.4 us: on_device(): jnp.einsum('td,fd->tf', grad_down_b, down_back, preferred_element_type=f32)]
    all_gather x4 -> x0, blocking collectives: 44.1 us -> none  [the longest x2 22.4 us: on_device(): lax.all_gather(keys_own, 'dp', axis=0, tiled=True)]
    unnamed x293 -> x43, local copies, waits for them, and re-layouts: 36.7 us -> 10.6 us
    another operation x4 -> x0, local copies, waits for them, and re-layouts: 19 us -> none  [the longest x3 18.2 us: one_scatter(): lines = jnp.concatenate([b.reshape(peers, -1) for b in blocks], axis=1)]
  transfers between devices with their start and end apart: 7 -> 0, of which waited for: 5 -> 0; matrix products, arithmetic and copies ran while one was open for 21% -> 0% of each run, Pallas kernels for 0% -> 0%
where the time goes in v1:
time: 186 us
  Pallas kernels  170 us (91%)
  local copies, waits for them, and re-layouts  15.2 us (8%)
    pallas_call x1, Pallas kernels, on_device(): pl.pallas_call(kernel, out_shape=(s(2, 256, D, dtype=BF), s(2, 256, D), s...  170 us
    unnamed x43, local copies, waits for them, and re-layouts  10.6 us
    concatenate x1, local copies, waits for them, and re-layouts, on_device(): jnp.concatenate([gain_attn_in, gain_attn_out, gain_query, gain_key, gain_...  4.1 us

profile of v1, /device:TPU:1, one launch (start us, length us, event | category | flops | bytes accessed | tf_op | source)
XLA Modules:
  0.0 186.0 jit_solution(13385619683454204343)
XLA Ops:
  0.6 4.1 %concatenate.3 = bf16[24]{0:T(256)(128)(2,1)S(1)} concatenate(bf16[5]{0:T(256)(128)(2,1)} %param.23, bf16[5]{0:T(256)(128)(2,1)} %param.24, bf16[2]{0:T(256)(128)(2,1)} %param.25, bf16[2]{0:T(256)(128)(2,1)} %param.26, bf16[5]{0:T(256)(128)(2,1)} %param.30, bf16[5]{0:T(256)(128)(2,1)} %param.31), dimensions={0} | concatenate | bytes 96 | tf_op jit(solution)/shard_map/concatenate | solution.py:795
  4.7 0.5 pad_bitcast_fusion.gains
  5.3 170.1 %block.1 = (bf16[2,256,640]{2,1,0:T(8,128)(2,1)}, f32[2,256,640]{2,1,0:T(8,128)}, f32[5,1024]{1,0:T(8,128)}, f32[5,256]{1,0:T(8,128)}, f32[5,256]{1,0:T(8,128)},...) custom-call(bf16[2,256,640]{2,1,0:T(8,128)(2,1)} %tok.1, ...), custom_call_target="tpu_custom_call" | custom-call | tf_op jit(solution)/shard_map/block/pallas_call | solution.py:804
  175.4 0.0 copy-start
  175.4 2.1 %copy.46 = bf16[2,256,640]{2,1,0:T(8,128)(2,1)} copy(bf16[2,256,640]{2,1,0:T(8,128)(2,1)} %get-tuple-element.60) | data formatting | bytes 1310720
  177.5 0.0 copy-done
  177.5 0.0 copy-start.5
  177.6 1.1 copy.47
  178.6 0.6 copy.48
  179.3 0.6 copy.49
  179.9 0.0 copy-done.6
  179.9 0.6 copy.50
  180.5 0.0 copy-done.5
  180.5 0.6 copy.51
  181.1 0.5 copy.52
  181.6 0.5 copy.53
  182.1 0.5 copy.54
  182.6 0.5 copy.55
  183.1 0.0 copy-done.2
  183.1 0.6 copy.56
  183.8 0.6 copy.57
  184.4 0.6 copy.58
  185.0 0.5 copy.59
  185.5 0.5 copy.60
  (22 shorter events, 0.0 us)
Async XLA Ops:
  175.4 2.1 %copy-start = (f32[2,256,640]{2,1,0:T(8,128)S(1)}, f32[2,256,640]{2,1,0:T(8,128)}, u32[]{:S(2)}) copy-start(f32[2,256,640]{2,1,0:T(8,128)} %get-tuple-element.61) | copy-start | bytes 3932164
  177.5 1.2 copy-start.4
  177.5 1.8 copy-start.7
  177.5 2.4 %copy-start.6 = (f32[5,256]{1,0:T(8,128)S(1)}, f32[5,256]{1,0:T(8,128)}, u32[]{:S(2)}) copy-start(f32[5,256]{1,0:T(8,128)} %get-tuple-element.64) | copy-start | bytes 15364
  177.5 3.0 %copy-start.5 = (f32[8,640]{1,0:T(8,128)S(1)}, f32[8,640]{1,0:T(8,128)}, u32[]{:S(2)}) copy-start(f32[8,640]{1,0:T(8,128)} %get-tuple-element.65) | copy-start | bytes 61444
  177.5 3.6 %copy-start.13 = (f32[1,5]{1,0:T(1,128)S(1)}, f32[1,5]{1,0:T(1,128)}, u32[]{:S(2)}) copy-start(f32[1,5]{1,0:T(1,128)} %get-tuple-element.36) | copy-start | bytes 64
  177.5 4.1 %copy-start.12 = (f32[1,5]{1,0:T(1,128)S(1)}, f32[1,5]{1,0:T(1,128)}, u32[]{:S(2)}) copy-start(f32[1,5]{1,0:T(1,128)} %get-tuple-element.37) | copy-start | bytes 64
  177.5 4.6 %copy-start.11 = (f32[1,2]{1,0:T(1,128)S(1)}, f32[1,2]{1,0:T(1,128)}, u32[]{:S(2)}) copy-start(f32[1,2]{1,0:T(1,128)} %get-tuple-element.38) | copy-start | bytes 28
  177.5 5.1 %copy-start.10 = (f32[1,2]{1,0:T(1,128)S(1)}, f32[1,2]{1,0:T(1,128)}, u32[]{:S(2)}) copy-start(f32[1,2]{1,0:T(1,128)} %get-tuple-element.39) | copy-start | bytes 28
  177.5 5.6 %copy-start.2 = (f32[5,2048]{1,0:T(8,128)S(1)}, f32[5,2048]{1,0:T(8,128)}, u32[]{:S(2)}) copy-start(f32[5,2048]{1,0:T(8,128)} %get-tuple-element.70) | copy-start | bytes 122884
  177.5 6.2 %copy-start.1 = (f32[5,2048]{1,0:T(8,128)S(1)}, f32[5,2048]{1,0:T(8,128)}, u32[]{:S(2)}) copy-start(f32[5,2048]{1,0:T(8,128)} %get-tuple-element.71) | copy-start | bytes 122884
  177.5 6.8 %copy-start.3 = (f32[16,640]{1,0:T(8,128)S(1)}, f32[16,640]{1,0:T(8,128)}, u32[]{:S(2)}) copy-start(f32[16,640]{1,0:T(8,128)} %get-tuple-element.72) | copy-start | bytes 122884
  177.6 7.5 %copy-start.9 = (f32[1,5]{1,0:T(1,128)S(1)}, f32[1,5]{1,0:T(1,128)}, u32[]{:S(2)}) copy-start(f32[1,5]{1,0:T(1,128)} %get-tuple-element.43) | copy-start | bytes 64
  177.6 8.0 %copy-start.8 = (f32[1,5]{1,0:T(1,128)S(1)}, f32[1,5]{1,0:T(1,128)}, u32[]{:S(2)}) copy-start(f32[1,5]{1,0:T(1,128)} %get-tuple-element.44) | copy-start | bytes 64

commit v2 on v1

v2 whole, which is shorter than its diff:
```python
import functools
import math

import jax
import jax.numpy as jnp
from jax import lax
from jax.experimental import pallas as pl
from jax.experimental.pallas import tpu as pltpu
from jax.sharding import PartitionSpec as P

MESH = pl.DeviceIdType.MESH
F32 = jnp.float32
BF = jnp.bfloat16
I32 = jnp.int32
EPS = 1e-06
THETA = 1000000.0
T = 512
D = 640
GAINS = ((0, 5, 640), (5, 5, 640), (10, 2, 256), (12, 2, 256), (14, 5, 640), (19, 5, 640))
N_SEM = 96


def mm(a, b):
    return lax.dot_general(a, b, (((1,), (0,)), ((), ())), preferred_element_type=F32)


def mm_nt(a, b):
    return lax.dot_general(a, b, (((1,), (1,)), ((), ())), preferred_element_type=F32)


def mm_tn(a, b):
    return lax.dot_general(a, b, (((0,), (0,)), ((), ())), preferred_element_type=F32)


def mean_last(v):
    return jnp.mean(v, -1, keepdims=True)


def inv_rms(v):
    return lax.rsqrt(mean_last(v * v) + EPS)


def iota(shape, dim):
    return lax.broadcasted_iota(I32, shape, dim)


def norm_back(v, gain, grad):
    r = inv_rms(v)
    hat = v * r
    gg = grad * gain
    return r * (gg - hat * mean_last(gg * hat)), grad * hat


def kernel(
    tok, cot, dl, n0, n1, n2, n3, n4, n5, wq, wk, wv, wo, wg, wu, wd,
    o_layer, o_gx, o_cols, o_rows,
    W1, W2, W3, W4, W5, GW, stf, stage, R1, mf, po, PR, DLB,
    XB, CB, NRM, NRMT, NFT, AMT, CS, SN, DCOL, DROW, GV, QR, Q, KR, KV, AM, LI, OA, LA, BR, HID, NF, GT, UT, HM, ACC, GD, LO,
    DAM, DD, DKV, DKR,
    G2, G3, G4, G5, C1, C2, C3, C4, C5, A1a, A1b, A2, A3, A4, A5, B1a, B1b, B2, B3, B4, B5,
    E1, E2, E3, E4, E5, GG, GGR, F2, c4f, R4, MISC, ss, rs, ls,
):
    f = lax.axis_index("fsdp")
    y = lax.axis_index("dp")
    x = f // 8
    z = (f // 2) % 4
    c = f % 2
    zh, zl = z // 2, z % 2
    me = {"x": x, "z": z, "c": c, "y": y}
    gi = c * 8 + zl * 4 + y
    ge = zl * 8 + c * 4 + y

    def dev(co):
        return ((co["x"] * 4 + co["z"]) * 2 + co["c"], co["y"])

    def member(j):
        return {"x": x, "z": zh * 2 + (j // 4) % 2, "c": j // 8, "y": j % 4}

    def moved(axis, k):
        co = dict(me)
        co[axis] = (me[axis] + k) % (2 if axis == "c" else 4)
        return co

    def near_y():
        return dict(me, y=y + 1 - 2 * (y % 2))

    def under(cond, fn):
        if cond is None:
            fn()
        else:
            pl.when(cond)(fn)

    count = [0]

    def fresh():
        count[0] += 1
        assert count[0] <= N_SEM
        return count[0] - 1

    sent = []

    def remote(src, dst, i, co):
        return pltpu.make_async_remote_copy(
            src_ref=src, dst_ref=dst, send_sem=ss.at[i], recv_sem=rs.at[i], device_id=dev(co), device_id_type=MESH
        )

    def post(copies, come, gone=None):
        i = fresh()
        for cond, src, dst, co in copies:
            under(cond, lambda src=src, dst=dst, co=co: remote(src, dst, i, co).start())
        sent.append((i, come if gone is None else gone))
        return [(i, come)]

    def send(src, dst, co):
        return post([(None, src, dst, co)], [(None, dst)])

    def arrived(batches):
        for i, come in batches:
            for cond, ref in come:
                under(cond, lambda i=i, ref=ref: remote(ref, ref, i, moved("c", 1)).wait_recv())

    def all_gone(batches):
        for i, gone in batches:
            for cond, ref in gone:
                under(cond, lambda i=i, ref=ref: remote(ref, ref, i, moved("c", 1)).wait_send())
        batches.clear()

    def sl_cols(r0, rn):
        def sl(co, done, width=1024):
            xs = slice(None) if "x" in done else pl.ds(co["x"], 1)
            zs = slice(None) if "z" in done else pl.ds(co["z"] // 2, 1)
            if "y" not in done:
                cs, w = co["c"] * 1024 + (co["z"] % 2) * 512 + co["y"] * 128, 128
            elif "z" not in done:
                cs, w = co["c"] * 1024 + (co["z"] % 2) * 512, 512
            else:
                cs, w = co["c"] * 1024, width
            return (xs, zs, pl.ds(r0, rn), pl.ds(pl.multiple_of(cs, 128), w))
        return sl

    def sl_out(co, done):
        xs = slice(None) if "x" in done else pl.ds(co["x"], 1)
        zs = slice(None) if "z" in done else pl.ds(co["z"], 1)
        if "y" in done:
            return (xs, zs, pl.ds(co["c"], 1), pl.ds(0, 32), pl.ds(0, 768))
        return (
            xs, zs, pl.ds(co["c"], 1),
            pl.ds(pl.multiple_of((co["y"] // 2) * 16, 16), 16), pl.ds(pl.multiple_of((co["y"] % 2) * 384, 128), 384),
        )

    def sl_down(co, done):
        xs = slice(None) if "x" in done else pl.ds(co["x"], 1)
        zs = slice(None) if "z" in done else pl.ds(co["z"], 1)
        rows = pl.ds(0, 64) if "y" in done else pl.ds(pl.multiple_of(co["y"] * 16, 16), 16)
        return (xs, zs, pl.ds(co["c"], 1), rows, pl.ds(0, 640))

    pieces = {
        "1": (W1, W2, sl_cols(0, 80), "yzx", (E1, None, None, C1)),
        "1a": (W1, W2, sl_cols(0, 48), "yzx", (None, B1a, A1a, None)),
        "1b": (W1, W2, sl_cols(48, 32), "yxz", (None, B1b, A1b, None)),
        "2": (W2, G2, sl_cols(0, 80), "yzx", (E2, B2, A2, C2)),
        "3": (W3, G3, sl_cols(0, 80), "yxz", (E3, B3, A3, C3)),
        "4": (W4, G4, sl_out, "zxy", (E4, B4, A4, C4)),
        "5": (W5, G5, sl_down, "xzy", (E5, B5, A5, C5)),
    }
    real = jnp.logical_or(c == 0, zl == 0)
    c0, c1 = c == 0, c == 1

    def gather(name, phase):
        w, _, sl, order, bufs = pieces[name]
        done = order[:phase]
        if name[0] == "1" and phase >= 2:
            wide, half = w.at[sl(me, done)], w.at[sl(me, done, 512)]
            if phase == 3:
                to = moved("c", 1)
                return post([(c0, wide, wide, to), (c1, half, half, to)], [(c0, half), (c1, wide)], [(c0, wide), (c1, half)])
            if order[2] == "z":
                ref = w.at[sl(me, done)]
                return post1z(name, phase, ref)
            to = [moved(order[phase], k) for k in (1, 2, 3)]
            b = bufs[phase]
            come = [(c0, b), (c1, b.at[:, :, :, :, pl.ds(0, 512)])]
            return post([(c0, wide, wide, t) for t in to] + [(c1, half, half, t) for t in to], come)
        ref = w.at[sl(me, done)]
        if phase == 3:
            return send(ref, ref, moved("c", 1))
        if name[0] == "1" and order[phase] == "z":
            return post1z(name, phase, ref)
        cond = real if name[0] == "1" else None
        copies = [(cond, ref, ref, moved(order[phase], k)) for k in (1, 2, 3)]
        return post(copies, [(cond, bufs[phase])])

    def post1z(name, phase, ref):
        b = pieces[name][4][phase]
        come = [
            (c0, b), (jnp.logical_and(c1, zl == 0), b.at[pl.ds(0, 1)]), (jnp.logical_and(c1, zl == 1), b.at[pl.ds(0, 2)]),
        ]
        return post([(real, ref, ref, moved("z", k)) for k in (1, 2, 3)], come, [(real, b)])

    bar = pltpu.get_barrier_semaphore()
    friends = [member((gi + d) % 16) for d in range(1, 16)]
    friends += [moved("z", 2)] + [dict(me, z=(zh * 2 + 2) % 4 + (1 - zl))] + [moved("x", k) for k in (1, 2, 3)]
    for co in friends:
        pl.semaphore_signal(bar, inc=1, device_id=dev(co), device_id_type=MESH)

    lane = iota((1, 128), 1)
    grow = jnp.zeros((1, 128), F32)
    for ref, (at, per, _) in zip((n0, n1, n2, n3, n4, n5), GAINS):
        own = ref[...].astype(F32)
        for r in range(per):
            grow = jnp.where(lane == at + r, own[0:1, r:r + 1], grow)
    for j in range(16):
        cols = slice(128 * j, 128 * j + 128)
        if j < 8:
            part = wq[:, cols]
        elif j < 10:
            part = wk[:, 128 * (j - 8):128 * (j - 7)]
        elif j < 12:
            part = wv[:, 128 * (j - 10):128 * (j - 9)]
        else:
            part = None
        stf[j, 0:5, :] = jnp.zeros((5, 128), F32) if part is None else part.astype(F32)
        stf[j, 5:10, :] = wg[:, cols].astype(F32)
        stf[j, 10:15, :] = wu[:, cols].astype(F32)
        stf[j, 15:16, :] = grow
    stage[...] = stf[...].astype(BF)
    wof = wo[...].astype(F32)
    twice = jnp.concatenate([wof, wof], axis=0)
    keep = (iota((16, 640), 0) // 8) == (y % 2)
    twice = jnp.where(keep, twice, 0.0).astype(BF)
    po[0, :, :] = twice[:, 0:384]
    po[1, :, 0:256] = twice[:, 384:640]
    po[1, :, 256:384] = jnp.zeros((16, 128), BF)
    rowid = iota((8, 128), 0)
    tile = jnp.zeros((8, 128), I32)
    for k in range(6):
        tile = jnp.where(rowid == k, dl[0, k // 3:k // 3 + 1, k % 3:k % 3 + 1], tile)
    DLB[c] = tile
    W5[x, z, c, pl.ds(pl.multiple_of(y * 16, 16), 16), :] = wd[...]

    pl.semaphore_wait(bar, len(friends))

    core_to = ((y + 1) // 2) % 2
    blocks = (c, 3 - c)
    micro = y // 2

    def either(v, fn):
        for k in (0, 1):
            pl.when(v == k)(lambda k=k: fn(k))

    def reorder(src, dst, to, mine_in, slot_of):
        i = (fresh(), fresh())
        away = []
        for k in (0, 1):
            own = jnp.logical_and(to[k]["c"] == c, to[k]["y"] == y)
            far = jnp.logical_not(own)

            def start_far(s, k=k):
                pltpu.make_async_remote_copy(
                    src_ref=src.at[k], dst_ref=dst.at[s], send_sem=ss.at[i[k]], recv_sem=rs.at[i[s]],
                    device_id=dev(to[k]), device_id_type=MESH,
                ).start()

            def copy_own(s, k=k):
                cp = pltpu.make_async_copy(src.at[k], dst.at[s], ls)
                cp.start()
                cp.wait()

            for s in (0, 1):
                pl.when(jnp.logical_and(far, slot_of[k] == s))(lambda s=s, f=start_far: f(s))
            for s in (0, 1):
                pl.when(jnp.logical_and(own, slot_of[k] == s))(lambda s=s, f=copy_own: f(s))
            away.append((i[k], [(far, src.at[k])]))
        sent.extend(away)
        return [(i[k], [(jnp.logical_not(mine_in[k]), dst.at[k])]) for k in (0, 1)]

    def reshard(src, dst):
        to = [dict(me, c=core_to, y=c + 2 * m) for m in (0, 1)]
        mine = [jnp.logical_and(blocks[s] == y, c == y % 2) for s in (0, 1)]
        return reorder(src, dst, to, mine, (micro, micro))

    def unshard(src, dst):
        to = [dict(me, c=y % 2, y=blocks[s]) for s in (0, 1)]
        mine = [jnp.logical_and(core_to == c, y == c + 2 * m) for m in (0, 1)]
        return reorder(src, dst, to, mine, (micro, micro))

    others = [(gi + d) % 16 for d in range(1, 16)]
    a2a = post([(None, stage.at[j], R1.at[ge], member(j)) for j in others], [(None, R1.at[pl.ds(0, 15)])])
    R1[ge] = stage[gi]
    pair = send(po.at[1 - y % 2], PR, near_y())
    lens_cp = send(DLB.at[c], DLB.at[c], moved("c", 1))
    g5 = gather("5", 0)

    arrived(a2a)
    for e in range(16):
        v = R1[e].astype(F32)
        for k in range(3):
            mf[k, 5 * e:5 * e + 5, :] = v[5 * k:5 * k + 5, :]
        mf[3, e:e + 1, :] = v[15:16, :]
    own_cols = pl.ds(pl.multiple_of(c * 1024 + zl * 512 + y * 128, 128), 128)
    W1[x, zh, :, own_cols] = mf[0].astype(BF)
    g1 = gather("1", 0)
    GW[x, zh] = mf[3, 0:16, :].astype(BF)
    gz = send(GW.at[x, zh], GW.at[x, zh], moved("z", 2))
    for w, k in ((W2, 1), (W3, 2)):
        w[x, zh, :, own_cols] = mf[k].astype(BF)
    arrived(pair)
    W4[x, z, c, pl.ds(pl.multiple_of((y // 2) * 16, 16), 16), pl.ds(pl.multiple_of((y % 2) * 384, 128), 384)] = (
        po[y % 2].astype(F32) + PR[...].astype(F32)
    ).astype(BF)
    g4, g2, g3 = gather("4", 0), gather("2", 0), gather("3", 0)
    arrived(g1)
    g1a, g1b = gather("1a", 1), gather("1b", 1)
    x_in = reshard(tok, XB)
    arrived(gz)
    gx = post([(None, GW.at[x], GW.at[x], moved("x", k)) for k in (1, 2, 3)], [(None, GW.at[pl.ds(0, 3)])])
    arrived(g5)
    g5 = gather("5", 1)
    arrived(g4)
    g4 = gather("4", 1)
    arrived(g2)
    g2 = gather("2", 1)
    arrived(g3)
    g3 = gather("3", 1)

    def doc_rows():
        lt = DLB[y % 2]
        first = y // 2 == 0
        l0 = jnp.where(first, lt[0:1, :], lt[3:4, :])[:, 0:1]
        l1 = jnp.where(first, lt[1:2, :], lt[4:5, :])[:, 0:1]
        return l0, l0, l1, l0 + l1

    def angles(s):
        l0, e0, l1, e1 = doc_rows()
        freq = jnp.exp(iota((1, 128), 1).astype(F32) * (-2.0 * math.log(THETA) / 256))
        t = blocks[s] * 256 + iota((256, 1), 0)
        p0, p1 = (t >= e0).astype(I32), (t >= e1).astype(I32)
        DCOL[s] = p0 + p1
        turned = (t - p0 * l0 - p1 * l1).astype(F32) * freq
        CS[s] = jnp.cos(turned)
        SN[s] = jnp.sin(turned)

    arrived(lens_cp)
    l0, e0, l1, e1 = doc_rows()
    for k in range(4):
        t = 256 * k + iota((1, 256), 1)
        DROW[k] = (t >= e0).astype(I32) + (t >= e1).astype(I32)
    arrived(g1a + g1b)
    g1a, g1b = gather("1a", 2), gather("1b", 2)
    angles(0)
    arrived(g4)
    g4 = gather("4", 2)
    arrived(gx)

    packed = GW[...].reshape(128, 128)
    for k, (lane, per, width) in enumerate(GAINS):
        col = iota((128, width), 1)
        shard = iota((128, width), 0)
        colf = col.astype(F32)
        rest = colf - per * jnp.floor((colf + 0.5) * (1.0 / per))
        pick = jnp.where(shard.astype(F32) == rest + lane, 1.0, 0.0).astype(BF)
        spread = mm(packed, pick)
        mine = jnp.logical_and(col >= per * shard, col < per * shard + per)
        GV[k:k + 1, 0:width] = jnp.sum(jnp.where(mine, spread, 0.0), 0, keepdims=True)

    def rows(n, fn):
        def step(i, carry):
            fn(pl.ds(pl.multiple_of(i * n, n), n))
            return carry
        lax.fori_loop(0, T // n, step, 0)

    xv = XB.reshape(T, D)
    cv = CB.reshape(T, D)
    csv, snv = CS.reshape(T, 128), SN.reshape(T, 128)

    def do_norm(r):
        v = xv[r, :].astype(F32)
        NRM[r, :] = (v * inv_rms(v) * GV[0:1, :]).astype(BF)
    arrived(x_in)
    rows(128, do_norm)
    arrived(g2)
    g2 = gather("2", 2)
    arrived(g3)
    g3 = gather("3", 2)
    arrived(g5)
    g5 = gather("5", 2)
    NRMT[...] = NRM[...].T
    angles(1)
    arrived(g1a + g1b)
    g1 = gather("1", 3)
    arrived(g1)

    def w1_cols(start, width):
        return W1[:, :, :, pl.ds(pl.multiple_of(start, 128), width)].reshape(D, width)

    def turn(u, cs, sn):
        u1, u2 = u[:, 0:128], u[:, 128:256]
        return u1 * cs - u2 * sn, u2 * cs + u1 * sn

    def turn_back(u, cs, sn):
        u1, u2 = u[:, 0:128], u[:, 128:256]
        return jnp.concatenate([u1 * cs + u2 * sn, u2 * cs - u1 * sn], -1)

    raw = mm(NRM[...], w1_cols(1024, 256))
    KR[...] = raw
    o1, o2 = turn(raw * inv_rms(raw) * GV[3:4, 0:256], csv[...], snv[...])
    vals = mm(NRM[...], w1_cols(1280, 256))
    for s in range(2):
        r = slice(256 * s, 256 * s + 256)
        KV[blocks[s], :, 0:128] = o1[r].astype(BF)
        KV[blocks[s], :, 128:256] = o2[r].astype(BF)
        KV[blocks[s], :, 256:512] = vals[r].astype(BF)
    kv_cp = sum([send(KV.at[blocks[s]], KV.at[blocks[s]], moved("c", 1)) for s in range(2)], [])

    def do_query(h, carry):
        raw = mm(NRM[...], w1_cols(h * 256, 256))
        QR[h] = raw.astype(BF)
        o1, o2 = turn(raw * inv_rms(raw) * GV[2:3, 0:256], csv[...], snv[...])
        for s in range(2):
            r = slice(256 * s, 256 * s + 256)
            Q[s, h, :, 0:128] = (o1[r] * 0.0625).astype(BF)
            Q[s, h, :, 128:256] = (o2[r] * 0.0625).astype(BF)
        return carry
    lax.fori_loop(0, 4, do_query, 0)

    arrived(kv_cp)

    def seen(s, kb):
        t = blocks[s] * 256 + iota((256, 256), 0)
        k = kb * 256 + iota((256, 256), 1)
        return jnp.logical_and(DCOL[s] == DROW[kb], t >= k)

    for s in range(2):
        OA[...] = jnp.zeros_like(OA)
        LA[...] = jnp.zeros_like(LA)

        def forward(kb, carry, s=s):
            vis = seen(s, kb)
            keys, vals = KV[kb, :, 0:256], KV[kb, :, 256:512]
            for h in range(4):
                p = jnp.where(vis, jnp.exp(mm_nt(Q[s, h], keys)), 0.0)
                LA[h] += jnp.sum(p, -1, keepdims=True)
                OA[h] += mm(p.astype(BF), vals)
            return carry
        lax.fori_loop(0, blocks[s] + 1, forward, 0)
        for h in range(4):
            inv = 1.0 / LA[h]
            LI[s, :, h:h + 1] = inv
            mixed = (OA[h] * inv).astype(BF)
            AM[256 * s:256 * s + 256, 256 * h:256 * h + 256] = mixed
            AMT[256 * h:256 * h + 256, 256 * s:256 * s + 256] = mixed.T
    arrived(g4)
    g4 = gather("4", 3)
    c_in = reshard(cot, CB)
    arrived(g4)
    w4v = W4.reshape(1024, 768)
    w5v = W5.reshape(2048, 640)

    def do_out(r):
        b = mm(AM[r, :], w4v[:, 0:640])
        BR[r, :] = b.astype(BF)
        hid = xv[r, :].astype(F32) + b * inv_rms(b) * GV[1:2, :]
        HID[r, :] = hid
        NF[r, :] = (hid * inv_rms(hid) * GV[4:5, :]).astype(BF)
    rows(256, do_out)
    NFT[...] = NF[...].T
    arrived(g2 + g3)
    g2, g3 = gather("2", 3), gather("3", 3)
    arrived(g2 + g3)

    def cols_of(w, at, width):
        return w[:, :, :, pl.ds(pl.multiple_of(at, 128), width)].reshape(D, width)

    def do_ffn(n, carry):
        at = pl.ds(pl.multiple_of(n * 512, 512), 512)
        gate = mm(NF[...], cols_of(W2, n * 512, 512))
        up = mm(NF[...], cols_of(W3, n * 512, 512))
        GT[:, at] = gate.astype(BF)
        UT[:, at] = up.astype(BF)
        HM[:, at] = (jax.nn.gelu(gate, approximate=True) * up).astype(BF)
        return carry
    lax.fori_loop(0, 2, do_ffn, 0)
    arrived(g5)
    g5 = gather("5", 3)
    lax.fori_loop(2, 4, do_ffn, 0)
    arrived(g5)

    arrived(c_in)
    all_gone(sent)
    GG[...] = jnp.zeros_like(GG)
    lov = LO.reshape(T, D)

    def do_down(r):
        d = mm(HM[r, :], w5v[...])
        rd = inv_rms(d)
        hat = d * rd
        lov[r, :] = (HID[r, :] + hat * GV[5:6, :]).astype(BF)
        g = cv[r, :].astype(F32)
        gg = g * GV[5:6, :]
        GD[r, :] = (rd * (gg - hat * mean_last(gg * hat))).astype(BF)
        GG[5:6, :] += jnp.sum(g * hat, 0, keepdims=True)
    rows(256, do_down)
    lo_in = unshard(LO, o_layer)
    lo_sent = list(sent)
    sent.clear()

    def sum_core(name):
        _, g, sl, order, bufs = pieces[name]
        to, buf = moved("c", 1), bufs[3]
        if name == "1":
            part = pl.ds(0, 512)
            small = buf.at[:, :, :, part]
            copies = [(c0, g.at[sl(to, order, 512)], small, to), (c1, g.at[sl(to, order)], buf, to)]
            return post(copies, [(c0, buf), (c1, small)], [(c0, small), (c1, buf)])
        return send(g.at[sl(to, order)], buf, to)

    def add_in(name, idx, bufs, out=None):
        g = pieces[name][1]
        shape = bufs[0].shape
        n1 = shape[1]
        kind = BF if len(bufs) == 1 else F32

        def at(s, k):
            return pl.ds(k if s == slice(None) else s.start + k, 1)

        def step(i, carry):
            here = (at(idx[0], i // n1), at(idx[1], i % n1)) + tuple(idx[2:])
            tot = g[here].astype(kind)
            for b in bufs:
                tot = tot + b[pl.ds(i // n1, 1), pl.ds(i % n1, 1)].astype(kind)
            if out is None:
                g[here] = tot.astype(BF)
            else:
                out(tot)
            return carry
        if shape[0] * n1 == 1:
            step(0, 0)
        else:
            lax.fori_loop(0, shape[0] * n1, step, 0)

    def add_core(name, batch):
        arrived(batch)
        _, _, sl, order, bufs = pieces[name]
        add_in(name, sl(me, order), [bufs[3]])

    def sum_phase(name, phase):
        _, g, sl, order, bufs = pieces[name]
        axis, done, buf = order[phase], order[:phase], bufs[phase]
        peers = [(k, moved(axis, k)) for k in (1, 2, 3)]
        if name[0] == "1" and axis == "z":
            copies = []
            for k, co in peers:
                cond = jnp.logical_or(c0, (z + k) % 2 == 0)
                copies.append((cond, g.at[sl(co, done)], buf.at[k - 1], co))
            gone = [(c0, buf), (jnp.logical_and(c1, zl == 0), buf.at[pl.ds(0, 1)]),
                    (jnp.logical_and(c1, zl == 1), buf.at[pl.ds(0, 2)])]
            return post(copies, [(real, buf)], gone)
        if name[0] == "1" and phase == 2:
            part = pl.ds(0, 512)
            copies = [(c0, g.at[sl(co, done)], buf.at[k - 1], co) for k, co in peers]
            copies += [(c1, g.at[sl(co, done, 512)], buf.at[k - 1, :, :, :, part], co) for k, co in peers]
            return post(copies, [(c0, buf), (c1, buf.at[:, :, :, :, part])])
        cond = real if name[0] == "1" else None
        return post([(cond, g.at[sl(co, done)], buf.at[k - 1], co) for k, co in peers], [(cond, buf)])

    def add_phase(name, phase, batch, out=None):
        arrived(batch)
        _, _, sl, order, bufs = pieces[name]
        add_in(name, sl(me, order[:phase]), [bufs[phase].at[k] for k in range(3)], out)

    g5v = G5.reshape(2048, 640)

    def do_down_grad(n, carry):
        at = pl.ds(pl.multiple_of(n * 512, 512), 512)
        g5v[at, :] = mm_tn(HM[:, at], GD[...]).astype(BF)
        return carry
    lax.fori_loop(0, 4, do_down_grad, 0)
    s5 = sum_core("5")

    def do_ffn_back(n, carry):
        at = pl.ds(pl.multiple_of(n * 512, 512), 512)
        dh = mm_nt(GD[...], w5v[at, :])
        gate, up = GT[:, at].astype(F32), UT[:, at].astype(F32)
        k0, k1 = math.sqrt(2.0 / math.pi), 0.044715
        sq = gate * gate
        th = jnp.tanh(gate * (k0 + k0 * k1 * sq))
        half = 0.5 * (1.0 + th)
        slope = half + (0.5 * gate) * (1.0 - th * th) * (k0 + 3.0 * k0 * k1 * sq)
        dg = (dh * up * slope).astype(BF)
        du = (dh * (gate * half)).astype(BF)
        GT[:, at] = dg
        UT[:, at] = du
        G2[:, :, :, at] = mm(NFT[...], dg).astype(BF).reshape(4, 2, 80, 512)
        G3[:, :, :, at] = mm(NFT[...], du).astype(BF).reshape(4, 2, 80, 512)
        return carry
    lax.fori_loop(0, 1, do_ffn_back, 0)
    add_core("5", s5)
    s5 = sum_phase("5", 2)
    lax.fori_loop(1, 4, do_ffn_back, 0)
    s2, s3 = sum_core("2"), sum_core("3")

    def do_ffn_in(n, carry):
        at = pl.ds(pl.multiple_of(n * 512, 512), 512)
        both = mm_nt(GT[:, at], cols_of(W2, n * 512, 512)) + mm_nt(UT[:, at], cols_of(W3, n * 512, 512))
        if carry is None:
            ACC[...] = both
        else:
            ACC[...] += both
        return carry
    do_ffn_in(0, None)
    add_core("2", s2)
    s2 = sum_phase("2", 2)
    lax.fori_loop(1, 2, do_ffn_in, 0)
    add_core("3", s3)
    s3 = sum_phase("3", 2)
    lax.fori_loop(2, 4, do_ffn_in, 0)

    def do_mid(r):
        g = cv[r, :].astype(F32)
        dv, rowg = norm_back(HID[r, :], GV[4:5, :], ACC[r, :])
        GG[4:5, :] += jnp.sum(rowg, 0, keepdims=True)
        gh = g + dv
        HID[r, :] = gh
        db, rowo = norm_back(BR[r, :].astype(F32), GV[1:2, :], gh)
        GG[1:2, :] += jnp.sum(rowo, 0, keepdims=True)
        GD[r, :] = db.astype(BF)
    rows(128, do_mid)
    g4v = G4.reshape(1024, 768)

    for h in range(4):
        at = slice(256 * h, 256 * h + 256)
        g4v[at, 0:640] = mm(AMT[at, :], GD[...]).astype(BF)
        g4v[at, 640:768] = jnp.zeros((256, 128), BF)
        dam = mm_nt(GD[...], w4v[at, 0:640]).astype(BF)
        inner = jnp.sum(dam.astype(F32) * AM[:, at].astype(F32), -1, keepdims=True)
        for s in range(2):
            r = slice(256 * s, 256 * s + 256)
            DAM[s, h] = dam[r]
            DD[s, :, h:h + 1] = inner[r]
    s4 = sum_core("4")

    DKV[...] = jnp.zeros_like(DKV)
    for s in range(2):
        OA[...] = jnp.zeros_like(OA)

        def backward(kb, carry, s=s, progress={}):
            vis = seen(s, kb)
            keys, vals = KV[kb, :, 0:256], KV[kb, :, 256:512]
            dk = jnp.zeros((256, 256), F32)
            dv = jnp.zeros((256, 256), F32)
            for h in range(4):
                q, da = Q[s, h], DAM[s, h]
                p = jnp.where(vis, jnp.exp(mm_nt(q, keys)) * LI[s, :, h:h + 1], 0.0)
                ds = (p * (mm_nt(da, vals) - DD[s, :, h:h + 1])).astype(BF)
                OA[h] += mm(ds, keys)
                dk = dk + mm_tn(ds, q)
                dv = dv + mm_tn(p.astype(BF), da)
            DKV[kb, :, 0:256] += dk
            DKV[kb, :, 256:512] += dv
            for k, fn in progress.items():
                pl.when(kb == k)(fn)
            return carry
        held = {}

        def early():
            add_core("4", s4)
            held["4"] = sum_phase("4", 2)

        def one():
            add_phase("2", 2, s2)
            held["2"] = sum_phase("2", 1)

        def two():
            add_phase("3", 2, s3)
            held["3"] = sum_phase("3", 1)

        steps = {0: early} if s == 0 else {1: one, 2: two}
        lax.fori_loop(0, blocks[s] + 1, functools.partial(backward, progress=steps), 0)
        if s == 0:
            s4 = held["4"]
            add_phase("5", 2, s5)
            s5 = sum_phase("5", 1)
        else:
            s2, s3 = held["2"], held["3"]

        def query_back(h, carry, s=s):
            dq = turn_back(OA[h] * 0.0625, CS[s], SN[s])
            raw = QR[h, 256 * s:256 * s + 256, :].astype(F32)
            dv, rowg = norm_back(raw, GV[2:3, 0:256], dq)
            GG[2:3, 0:256] += jnp.sum(rowg, 0, keepdims=True)
            GT[256 * s:256 * s + 256, pl.ds(pl.multiple_of(h * 256, 256), 256)] = dv.astype(BF)
            return carry
        lax.fori_loop(0, 4, query_back, 0)
    for s in range(2):
        HM[256 * s:256 * s + 256, 0:512] = DKV[1 - c if s == 0 else 2 + c].astype(BF)
    dk_cp = send(HM.at[:, pl.ds(0, 512)], DKR, moved("c", 1))

    def do_qkv_grad(n, carry):
        at = pl.ds(pl.multiple_of(n * 512, 512), 512)
        W2[:, :, :, at] = mm(NRMT[...], GT[:, at]).astype(BF).reshape(4, 2, 80, 512)
        return carry
    lax.fori_loop(0, 2, do_qkv_grad, 0)
    arrived(dk_cp)
    for s in range(2):
        r = slice(256 * s, 256 * s + 256)
        tot = DKV[blocks[s]] + DKR[r, :].astype(F32)
        dk = turn_back(tot[:, 0:256], CS[s], SN[s])
        dv, rowg = norm_back(KR[r, :], GV[3:4, 0:256], dk)
        GG[3:4, 0:256] += jnp.sum(rowg, 0, keepdims=True)
        GT[r, 1024:1280] = dv.astype(BF)
        GT[r, 1280:1536] = tot[:, 256:512].astype(BF)
    do_qkv_grad(2, 0)
    s1 = sum_core("1")

    def do_dnorm(n, carry):
        at = pl.ds(pl.multiple_of(n * 512, 512), 512)
        part = mm_nt(GT[:, at], w1_cols(n * 512, 512))
        if carry is None:
            ACC[...] = part
        else:
            ACC[...] += part
        return carry
    do_dnorm(0, None)
    add_core("1", s1)
    s1a, s1b = sum_phase("1a", 2), sum_phase("1b", 2)
    add_phase("5", 1, s5)
    s5 = sum_phase("5", 0)
    lax.fori_loop(1, 3, do_dnorm, 0)
    all_gone(lo_sent)
    gxv = LO.reshape(T, D)

    def do_x(r):
        dv, rowg = norm_back(xv[r, :].astype(F32), GV[0:1, :], ACC[r, :])
        GG[0:1, :] += jnp.sum(rowg, 0, keepdims=True)
        gxv[r, :] = (HID[r, :] + dv).astype(BF)
    rows(128, do_x)
    gx_in = unshard(LO, o_gx)
    add_phase("4", 2, s4)
    s4 = sum_phase("4", 1)

    gcp = send(GG, GGR.at[0], moved("c", 1))
    add_phase("2", 1, s2)
    s2 = sum_phase("2", 0)
    add_phase("3", 1, s3)
    s3 = sum_phase("3", 0)

    def out_down(v):
        MISC[0:16, :] = v.reshape(16, 640)
    add_phase("5", 0, s5, out_down)
    arrived(gcp)
    base = 1
    tot = GG[...] + GGR[0]

    def gain_step(a, axis):
        GGR[10 + a] = tot
        return post(
            [(None, GGR.at[10 + a], GGR.at[base + 3 * a + k - 1], moved(axis, k)) for k in (1, 2, 3)],
            [(None, GGR.at[pl.ds(base + 3 * a, 3)])],
        )

    def gain_sum(a, tot):
        for k in range(3):
            tot = tot + GGR[base + 3 * a + k]
        return tot

    gs = gain_step(0, "z")
    add_phase("4", 1, s4)
    s4 = sum_phase("4", 0)
    arrived(gs)
    tot = gain_sum(0, tot)
    gs = gain_step(1, "y")

    add_phase("1a", 2, s1a)
    s1a = sum_phase("1a", 1)
    add_phase("1b", 2, s1b)
    s1b = sum_phase("1b", 1)

    def into(k):
        def out(v):
            mf[k] = v.reshape(80, 128)
        return out

    def out_4(v):
        c4f[...] = v.reshape(16, 384)

    arrived(gs)
    tot = gain_sum(1, tot)
    gs = gain_step(2, "x")
    add_phase("2", 0, s2, into(1))
    add_phase("3", 0, s3, into(2))
    add_phase("4", 0, s4, out_4)
    pair = send(c4f.at[pl.ds(pl.multiple_of(8 * (1 - y % 2), 8), 8), :], R4, near_y())
    for e in range(16):
        for k in (1, 2):
            F2[e, 5 * k:5 * k + 5, :] = mf[k, 5 * e:5 * e + 5, :]
    add_phase("1a", 1, s1a)
    add_phase("1b", 1, s1b)
    s1 = sum_phase("1", 0)
    arrived(gs)
    tot = gain_sum(2, tot)
    shard = f * 4 + y
    MISC[24:32, :] = jnp.zeros((8, D), F32)
    for k, (_, per, width) in enumerate(GAINS):
        line = tot[k:k + 1, 0:width]
        col = iota((1, width), 1)
        for r in range(per):
            MISC[24 + k:25 + k, r:r + 1] = jnp.sum(jnp.where(col == per * shard + r, line, 0.0), 1, keepdims=True)
    arrived(pair)
    own = c4f[pl.ds(pl.multiple_of(8 * (y % 2), 8), 8), :]
    left = y % 2 == 0
    MISC[16:24, 0:384] = jnp.where(left, own, R4[...])
    MISC[16:24, 384:640] = jnp.where(left, R4[...], own)[:, 0:256]
    keep_rows = pltpu.make_async_copy(MISC, o_rows, ls)
    keep_rows.start()
    keep_rows.wait()
    add_phase("1", 0, s1, into(0))
    for e in range(16):
        F2[e, 0:5, :] = mf[0, 5 * e:5 * e + 5, :]
    home = post(
        [(None, F2.at[(j // 4) % 2 * 8 + j // 8 * 4 + j % 4], o_cols.at[gi], member(j)) for j in others],
        [(None, o_cols.at[pl.ds(0, 15)])],
    )
    keep_cols = pltpu.make_async_copy(F2.at[ge], o_cols.at[gi], ls)
    keep_cols.start()
    keep_cols.wait()
    arrived(gx_in + lo_in + home)
    all_gone(sent)


def finish(lay, gx, cols, rows, o_layer, o_gx, o_q, o_k, o_v, o_o, o_gate, o_up, o_down, o0, o1, o2, o3, o4, o5):
    o_layer[...] = lay[...]
    for j in range(16):
        at = slice(128 * j, 128 * j + 128)
        v = cols[j]
        if j < 8:
            o_q[:, at] = v[0:5]
        elif j < 10:
            o_k[:, 128 * (j - 8):128 * (j - 7)] = v[0:5]
        elif j < 12:
            o_v[:, 128 * (j - 10):128 * (j - 9)] = v[0:5]
        o_gate[:, at] = v[5:10]
        o_up[:, at] = v[10:15]
    o_down[...] = rows[0:16, :]
    o_o[...] = rows[16:24, :]
    for k, ref in enumerate((o0, o1, o2, o3, o4, o5)):
        ref[...] = rows[24 + k:25 + k, 0:GAINS[k][1]]
    for m in range(2):
        o_gx[m] = gx[m].astype(F32)


def scratch():
    def v(*shape, dtype=F32):
        return pltpu.VMEM(shape, dtype)

    def b(*shape):
        return pltpu.VMEM(shape, BF)

    cols = (4, 2, 80, 2048)
    out = [
        b(*cols), b(*cols), b(*cols), b(4, 4, 2, 32, 768), b(4, 4, 2, 64, 640), b(4, 2, 16, 128),
        v(16, 16, 128), b(16, 16, 128), b(16, 16, 128), v(4, 80, 128), b(2, 16, 384), b(16, 384),
        v(2, 8, 128, dtype=I32),
        b(2, 256, D), b(2, 256, D), b(T, D), b(D, T), b(D, T), b(1024, T),
        v(2, 256, 128), v(2, 256, 128),
        v(2, 256, 1, dtype=I32), v(4, 1, 256, dtype=I32), v(8, D),
        b(4, T, 256), b(2, 4, 256, 256), v(T, 256), b(4, 256, 512), b(T, 1024),
        v(2, 256, 4), v(4, 256, 256), v(4, 256, 1),
        b(T, D), v(T, D), b(T, D), b(T, 2048), b(T, 2048), b(T, 2048), v(T, D), b(T, D),
        b(2, 256, D),
        b(2, 4, 256, 256), v(2, 256, 4), v(4, 256, 512), b(T, 512),
        b(*cols), b(*cols), b(4, 4, 2, 32, 768), b(4, 4, 2, 64, 640),
        b(4, 2, 80, 1024), b(4, 2, 80, 1024), b(4, 2, 80, 1024), b(4, 4, 1, 32, 768), b(4, 4, 1, 64, 640),
        b(3, 1, 2, 48, 1024), b(3, 4, 1, 32, 512), b(3, 1, 2, 80, 1024), b(3, 4, 1, 80, 512),
        b(3, 4, 4, 1, 16, 384), b(3, 4, 4, 1, 16, 640),
        b(3, 1, 1, 48, 512), b(3, 1, 1, 32, 512), b(3, 1, 1, 80, 512), b(3, 1, 1, 80, 512),
        b(3, 1, 4, 1, 16, 384), b(3, 4, 1, 1, 16, 640),
        b(3, 1, 1, 80, 128), b(3, 1, 1, 80, 128), b(3, 1, 1, 80, 128), b(3, 1, 1, 1, 16, 384), b(3, 1, 1, 1, 16, 640),
        v(8, D), v(13, 8, D), v(16, 16, 128), v(16, 384), v(8, 384), v(32, D),
        pltpu.SemaphoreType.DMA((N_SEM,)), pltpu.SemaphoreType.DMA((N_SEM,)), pltpu.SemaphoreType.DMA,
    ]
    return out


def on_device(tokens_in, cotangent, doc_lengths, w_query, w_key, w_value, w_out, gain_attn_in, gain_attn_out,
              gain_query, gain_key, w_gate, w_up, w_down, gain_ffn_in, gain_ffn_out):
    gains = [g.reshape(1, -1) for g in (gain_attn_in, gain_attn_out, gain_query, gain_key, gain_ffn_in, gain_ffn_out)]
    vm = pl.BlockSpec(memory_space=pltpu.VMEM)
    hbm = pl.BlockSpec(memory_space=pl.ANY)

    def s(*shape, dtype=F32):
        return jax.ShapeDtypeStruct(shape, dtype)

    parts = pl.pallas_call(
        kernel,
        out_shape=(s(2, 256, D, dtype=BF), s(2, 256, D, dtype=BF), s(16, 16, 128), s(32, D)),
        in_specs=[hbm, hbm] + [vm] * 14,
        out_specs=(hbm,) * 4,
        scratch_shapes=scratch(),
        compiler_params=pltpu.CompilerParams(
            collective_id=0, has_side_effects=True, vmem_limit_bytes=64 * 1024 * 1024 - 65536
        ),
        name="block",
    )(tokens_in, cotangent, doc_lengths, *gains, w_query, w_key, w_value, w_out, w_gate, w_up, w_down)
    outs = pl.pallas_call(
        finish,
        out_shape=(
            s(2, 256, D, dtype=BF), s(2, 256, D), s(5, 1024), s(5, 256), s(5, 256), s(8, D), s(5, 2048), s(5, 2048),
            s(16, D), s(1, 5), s(1, 5), s(1, 2), s(1, 2), s(1, 5), s(1, 5),
        ),
        in_specs=[vm] * 4,
        out_specs=(vm,) * 15,
        name="finish",
    )(*parts)
    (layer_out, grad_x, gq, gk, gv, go, ggate, gup, gdown, g0, g1, g2, g3, g4, g5) = outs
    return (
        layer_out, grad_x, gq, gk, gv, go, g0.reshape(-1), g1.reshape(-1), g2.reshape(-1), g3.reshape(-1),
        ggate, gup, gdown, g4.reshape(-1), g5.reshape(-1),
    )


def solution(mesh):
    both = ("fsdp", "dp")
    row, gain = P(both, None), P(both)
    tok = P(None, both, None)
    return jax.shard_map(
        on_device,
        mesh=mesh,
        in_specs=(tok, tok, P("fsdp", None, None), row, row, row, row, gain, gain, gain, gain, row, row, row, gain, gain),
        out_specs=(tok, tok, row, row, row, row, gain, gain, gain, gain, row, row, row, gain, gain),
        check_vma=False,
    )
```

time: 186 us -> 140 us (0.75)
  Pallas kernels: 170 us -> 138 us
  local copies, waits for them, and re-layouts: 15.2 us -> 0 us
    pallas_call x1 -> x2, Pallas kernels: 170 us -> 138 us  [the longest x1 136 us: on_device(): pl.pallas_call(kernel, out_shape=(s(2, 256, D, dtype=BF), s(2, 256, D, dt...]
    unnamed x43 -> x0, local copies, waits for them, and re-layouts: 10.6 us -> none
    concatenate x1 -> x0, local copies, waits for them, and re-layouts: 4.1 us -> none  [on_device(): jnp.concatenate([gain_attn_in, gain_attn_out, gain_query, gain_key, gain_...]
where the time goes in v2:
time: 140 us; the launch traced here: 139 us
  Pallas kernels  138 us (99%)
    pallas_call x1, Pallas kernels, on_device(): pl.pallas_call(kernel, out_shape=(s(2, 256, D, dtype=BF), s(2, 256, D, dt...  136 us

profile of v2, /device:TPU:1, one launch (start us, length us, event | category | flops | bytes accessed | tf_op | source)
XLA Modules:
  0.0 139.3 jit_solution(3017973167808372538)
XLA Ops:
  0.7 135.7 %block.1 = (bf16[2,256,640]{2,1,0:T(8,128)(2,1)}, bf16[2,256,640]{2,1,0:T(8,128)(2,1)}, f32[16,16,128]{2,1,0:T(8,128)}, f32[32,640]{1,0:T(8,128)}) custom-call(bf16[2,256,640]{2,1,0:T(8,128)(2,1)} %tok.1, bf16[2,256,640]{2,1,0:T(8,128)(2,1)} %cot.1, s32[1,2,3]{2,1,0:T(2,128)} %dl.1, bf16[1,5]{1,0:T(2,128)(2,1)} %bitcast.12, bf16[1,5]{1,0:T(2,128)(2,1)} %bitcast.13, ...), custom_call_target="tpu_custom_call" | custom-call | tf_op jit(solution)/shard_map/block/pallas_call | solution.py:893
  136.4 2.8 %finish.1 = (bf16[2,256,640]{2,1,0:T(8,128)(2,1)}, f32[2,256,640]{2,1,0:T(8,128)}, f32[5,1024]{1,0:T(8,128)}, f32[5,256]{1,0:T(8,128)}, f32[5,256]{1,0:T(8,128)}...) custom-call(bf16[2,256,640]{2,1,0:T(8,128)(2,1)} %get-tuple-element., ...), custom_call_target="tpu_custom_call" | custom-call | tf_op jit(solution)/shard_map/finish/pallas_call | solution.py:904

commit v3 on v2

--- a/solution.py
+++ b/solution.py
@@ -189,6 +189,21 @@
         cond = real if name[0] == "1" else None
         copies = [(cond, ref, ref, moved(order[phase], k)) for k in (1, 2, 3)]
         return post(copies, [(cond, bufs[phase])])
+
+    def ring(name, step):
+        w, _, sl, order, bufs = pieces[name]
+        axis, done, buf = order[2], order[:2], bufs[2]
+        right, left = moved(axis, 1), moved(axis, 3)
+        if step == 0:
+            ref = w.at[sl(me, done)]
+            return post([(None, ref, ref, right), (None, ref, ref, left)], [(None, buf.at[pl.ds(0, 2)])])
+
+        def half(co, k):
+            at = sl(co, done)
+            n = at[3].size // 2
+            return w.at[at[:3] + (pl.ds(pl.multiple_of(at[3].start + k * n, 128), n),)]
+        one, two = half(left, 0), half(right, 1)
+        return post([(None, one, one, right), (None, two, two, left)], [(None, buf.at[pl.ds(0, 1)])])
 
     def post1z(name, phase, ref):
         b = pieces[name][4][phase]
@@ -314,14 +329,18 @@
     x_in = reshard(tok, XB)
     arrived(gz)
     gx = post([(None, GW.at[x], GW.at[x], moved("x", k)) for k in (1, 2, 3)], [(None, GW.at[pl.ds(0, 3)])])
-    arrived(g5)
-    g5 = gather("5", 1)
+    arrived(g1a)
+    g1a = gather("1a", 2)
+    arrived(g1b)
+    g1b = gather("1b", 2)
     arrived(g4)
     g4 = gather("4", 1)
     arrived(g2)
     g2 = gather("2", 1)
     arrived(g3)
     g3 = gather("3", 1)
+    arrived(g5)
+    g5 = gather("5", 1)
 
     def doc_rows():
         lt = DLB[y % 2]
@@ -345,11 +364,8 @@
     for k in range(4):
         t = 256 * k + iota((1, 256), 1)
         DROW[k] = (t >= e0).astype(I32) + (t >= e1).astype(I32)
-    arrived(g1a + g1b)
-    g1a, g1b = gather("1a", 2), gather("1b", 2)
     angles(0)
-    arrived(g4)
-    g4 = gather("4", 2)
+    angles(1)
     arrived(gx)
 
     packed = GW[...].reshape(128, 128)
@@ -378,16 +394,17 @@
         NRM[r, :] = (v * inv_rms(v) * GV[0:1, :]).astype(BF)
     arrived(x_in)
     rows(128, do_norm)
+    arrived(g4)
+    g4 = gather("4", 2)
+    arrived(g1a + g1b)
+    g1 = gather("1", 3)
     arrived(g2)
-    g2 = gather("2", 2)
+    g2 = ring("2", 0)
     arrived(g3)
-    g3 = gather("3", 2)
+    g3 = ring("3", 0)
     arrived(g5)
     g5 = gather("5", 2)
     NRMT[...] = NRM[...].T
-    angles(1)
-    arrived(g1a + g1b)
-    g1 = gather("1", 3)
     arrived(g1)
 
     def w1_cols(start, width):
@@ -434,24 +451,38 @@
         OA[...] = jnp.zeros_like(OA)
         LA[...] = jnp.zeros_like(LA)
 
-        def forward(kb, carry, s=s):
+        def forward(kb, carry, s=s, progress={}):
             vis = seen(s, kb)
             keys, vals = KV[kb, :, 0:256], KV[kb, :, 256:512]
             for h in range(4):
                 p = jnp.where(vis, jnp.exp(mm_nt(Q[s, h], keys)), 0.0)
                 LA[h] += jnp.sum(p, -1, keepdims=True)
                 OA[h] += mm(p.astype(BF), vals)
+            for k, fn in progress.items():
+                pl.when(kb == k)(fn)
             return carry
-        lax.fori_loop(0, blocks[s] + 1, forward, 0)
+        held = {}
+
+        def core_four():
+            arrived(g4)
+            held["4"] = gather("4", 3)
+
+        def pass_on():
+            arrived(g2 + g3)
+            held["2"], held["3"] = ring("2", 1), ring("3", 1)
+
+        steps = {} if s == 0 else {1: core_four, 2: pass_on}
+        lax.fori_loop(0, blocks[s] + 1, functools.partial(forward, progress=steps), 0)
         for h in range(4):
             inv = 1.0 / LA[h]
             LI[s, :, h:h + 1] = inv
             mixed = (OA[h] * inv).astype(BF)
             AM[256 * s:256 * s + 256, 256 * h:256 * h + 256] = mixed
             AMT[256 * h:256 * h + 256, 256 * s:256 * s + 256] = mixed.T
-    arrived(g4)
-    g4 = gather("4", 3)
+    g4, g2, g3 = held["4"], held["2"], held["3"]
     c_in = reshard(cot, CB)
+    arrived(g2 + g3)
+    g2, g3 = gather("2", 3), gather("3", 3)
     arrived(g4)
     w4v = W4.reshape(1024, 768)
     w5v = W5.reshape(2048, 640)
@@ -464,8 +495,6 @@
         NF[r, :] = (hid * inv_rms(hid) * GV[4:5, :]).astype(BF)
     rows(256, do_out)
     NFT[...] = NF[...].T
-    arrived(g2 + g3)
-    g2, g3 = gather("2", 3), gather("3", 3)
     arrived(g2 + g3)
 
     def cols_of(w, at, width):
@@ -504,14 +533,15 @@
     lo_sent = list(sent)
     sent.clear()
 
-    def sum_core(name):
+    def sum_core(name, half=None):
         _, g, sl, order, bufs = pieces[name]
         to, buf = moved("c", 1), bufs[3]
-        if name == "1":
-            part = pl.ds(0, 512)
-            small = buf.at[:, :, :, part]
-            copies = [(c0, g.at[sl(to, order, 512)], small, to), (c1, g.at[sl(to, order)], buf, to)]
-            return post(copies, [(c0, buf), (c1, small)], [(c0, small), (c1, buf)])
+        if half == 0:
+            return post([(c1, g.at[sl(to, order)], buf, to)], [(c0, buf)], [(c1, buf)])
+        if half == 1:
+            wide = 512 if name == "1" else 1024
+            buf = buf.at[:, :, :, pl.ds(0, wide)]
+            return post([(c0, g.at[sl(to, order, wide)], buf, to)], [(c1, buf)], [(c0, buf)])
         return send(g.at[sl(to, order)], buf, to)
 
     def add_in(name, idx, bufs, out=None):
@@ -538,29 +568,32 @@
         else:
             lax.fori_loop(0, shape[0] * n1, step, 0)
 
-    def add_core(name, batch):
+    def add_core(name, batch, half=None):
         arrived(batch)
         _, _, sl, order, bufs = pieces[name]
-        add_in(name, sl(me, order), [bufs[3]])
-
-    def sum_phase(name, phase):
+        under(None if half is None else c == half, lambda: add_in(name, sl(me, order), [bufs[3]]))
+
+    def sum_phase(name, phase, half=None):
         _, g, sl, order, bufs = pieces[name]
         axis, done, buf = order[phase], order[:phase], bufs[phase]
         peers = [(k, moved(axis, k)) for k in (1, 2, 3)]
-        if name[0] == "1" and axis == "z":
+        if name[0] == "1" and axis == "z" and half != 0:
             copies = []
+            both = half is None
             for k, co in peers:
-                cond = jnp.logical_or(c0, (z + k) % 2 == 0)
+                even = (z + k) % 2 == 0
+                cond = jnp.logical_or(c0, even) if both else jnp.logical_and(c1, even)
                 copies.append((cond, g.at[sl(co, done)], buf.at[k - 1], co))
-            gone = [(c0, buf), (jnp.logical_and(c1, zl == 0), buf.at[pl.ds(0, 1)]),
-                    (jnp.logical_and(c1, zl == 1), buf.at[pl.ds(0, 2)])]
-            return post(copies, [(real, buf)], gone)
-        if name[0] == "1" and phase == 2:
+            gone = [(jnp.logical_and(c1, zl == 0), buf.at[pl.ds(0, 1)]),
+                    (jnp.logical_and(c1, zl == 1), buf.at[pl.ds(0, 2)])] + ([(c0, buf)] if both else [])
+            return post(copies, [(real if both else jnp.logical_and(c1, zl == 0), buf)], gone)
+        if name[0] == "1" and phase == 2 and half == 1:
             part = pl.ds(0, 512)
-            copies = [(c0, g.at[sl(co, done)], buf.at[k - 1], co) for k, co in peers]
-            copies += [(c1, g.at[sl(co, done, 512)], buf.at[k - 1, :, :, :, part], co) for k, co in peers]
-            return post(copies, [(c0, buf), (c1, buf.at[:, :, :, :, part])])
+            copies = [(c1, g.at[sl(co, done, 512)], buf.at[k - 1, :, :, :, part], co) for k, co in peers]
+            return post(copies, [(c1, buf.at[:, :, :, :, part])])
         cond = real if name[0] == "1" else None
+        if half is not None:
+            cond = c == half
         return post([(cond, g.at[sl(co, done)], buf.at[k - 1], co) for k, co in peers], [(cond, buf)])
 
     def add_phase(name, phase, batch, out=None):
@@ -593,11 +626,17 @@
         G2[:, :, :, at] = mm(NFT[...], dg).astype(BF).reshape(4, 2, 80, 512)
         G3[:, :, :, at] = mm(NFT[...], du).astype(BF).reshape(4, 2, 80, 512)
         return carry
-    lax.fori_loop(0, 1, do_ffn_back, 0)
+    lax.fori_loop(0, 2, do_ffn_back, 0)
+    s2, s3 = sum_core("2", 0), sum_core("3", 0)
     add_core("5", s5)
     s5 = sum_phase("5", 2)
-    lax.fori_loop(1, 4, do_ffn_back, 0)
-    s2, s3 = sum_core("2"), sum_core("3")
+    lax.fori_loop(2, 3, do_ffn_back, 0)
+    add_core("2", s2, 0)
+    s2 = sum_phase("2", 2, 0)
+    add_core("3", s3, 0)
+    s3 = sum_phase("3", 2, 0)
+    lax.fori_loop(3, 4, do_ffn_back, 0)
+    t2, t3 = sum_core("2", 1), sum_core("3", 1)
 
     def do_ffn_in(n, carry):
         at = pl.ds(pl.multiple_of(n * 512, 512), 512)
@@ -608,12 +647,11 @@
             ACC[...] += both
         return carry
     do_ffn_in(0, None)
-    add_core("2", s2)
-    s2 = sum_phase("2", 2)
-    lax.fori_loop(1, 2, do_ffn_in, 0)
-    add_core("3", s3)
-    s3 = sum_phase("3", 2)
-    lax.fori_loop(2, 4, do_ffn_in, 0)
+    add_core("2", t2, 1)
+    s2 = s2 + sum_phase("2", 2, 1)
+    add_core("3", t3, 1)
+    s3 = s3 + sum_phase("3", 2, 1)
+    lax.fori_loop(1, 4, do_ffn_in, 0)
 
     def do_mid(r):
         g = cv[r, :].astype(F32)
@@ -670,18 +708,14 @@
             add_phase("2", 2, s2)
             held["2"] = sum_phase("2", 1)
 
-        def two():
-            add_phase("3", 2, s3)
-            held["3"] = sum_phase("3", 1)
-
-        steps = {0: early} if s == 0 else {1: one, 2: two}
+        steps = {0: early} if s == 0 else {2: one}
         lax.fori_loop(0, blocks[s] + 1, functools.partial(backward, progress=steps), 0)
         if s == 0:
             s4 = held["4"]
             add_phase("5", 2, s5)
             s5 = sum_phase("5", 1)
         else:
-            s2, s3 = held["2"], held["3"]
+            s2 = held["2"]
 
         def query_back(h, carry, s=s):
             dq = turn_back(OA[h] * 0.0625, CS[s], SN[s])
@@ -700,6 +734,9 @@
         W2[:, :, :, at] = mm(NRMT[...], GT[:, at]).astype(BF).reshape(4, 2, 80, 512)
         return carry
     lax.fori_loop(0, 2, do_qkv_grad, 0)
+    s1 = sum_core("1", 0)
+    add_phase("3", 2, s3)
+    s3 = sum_phase("3", 1)
     arrived(dk_cp)
     for s in range(2):
         r = slice(256 * s, 256 * s + 256)
@@ -710,7 +747,9 @@
         GT[r, 1024:1280] = dv.astype(BF)
         GT[r, 1280:1536] = tot[:, 256:512].astype(BF)
     do_qkv_grad(2, 0)
-    s1 = sum_core("1")
+    t1 = sum_core("1", 1)
+    add_core("1", s1, 0)
+    s1a, s1b = sum_phase("1a", 2, 0), sum_phase("1b", 2, 0)
 
     def do_dnorm(n, carry):
         at = pl.ds(pl.multiple_of(n * 512, 512), 512)
@@ -721,11 +760,15 @@
             ACC[...] += part
         return carry
     do_dnorm(0, None)
-    add_core("1", s1)
-    s1a, s1b = sum_phase("1a", 2), sum_phase("1b", 2)
+    add_core("1", t1, 1)
+    s1a, s1b = s1a + sum_phase("1a", 2, 1), s1b + sum_phase("1b", 2, 1)
     add_phase("5", 1, s5)
     s5 = sum_phase("5", 0)
     lax.fori_loop(1, 3, do_dnorm, 0)
+    add_phase("2", 1, s2)
+    s2 = sum_phase("2", 0)
+    add_phase("3", 1, s3)
+    s3 = sum_phase("3", 0)
     all_gone(lo_sent)
     gxv = LO.reshape(T, D)
 
@@ -735,45 +778,21 @@
         gxv[r, :] = (HID[r, :] + dv).astype(BF)
     rows(128, do_x)
     gx_in = unshard(LO, o_gx)
-    add_phase("4", 2, s4)
-    s4 = sum_phase("4", 1)
-
-    gcp = send(GG, GGR.at[0], moved("c", 1))
-    add_phase("2", 1, s2)
-    s2 = sum_phase("2", 0)
-    add_phase("3", 1, s3)
-    s3 = sum_phase("3", 0)
-
-    def out_down(v):
-        MISC[0:16, :] = v.reshape(16, 640)
-    add_phase("5", 0, s5, out_down)
-    arrived(gcp)
-    base = 1
-    tot = GG[...] + GGR[0]
-
-    def gain_step(a, axis):
-        GGR[10 + a] = tot
+
+    near = [dict(me, c=(c + dc) % 2, y=(y + dy) % 4) for dc in (0, 1) for dy in range(4) if dc + dy > 0]
+    gs = post([(None, GG, GGR.at[i], co) for i, co in enumerate(near)], [(None, GGR.at[pl.ds(0, 7)])])
+
+    def gain_step(axis, base, tot):
+        GGR[base + 3] = tot
         return post(
-            [(None, GGR.at[10 + a], GGR.at[base + 3 * a + k - 1], moved(axis, k)) for k in (1, 2, 3)],
-            [(None, GGR.at[pl.ds(base + 3 * a, 3)])],
+            [(None, GGR.at[base + 3], GGR.at[base + k - 1], moved(axis, k)) for k in (1, 2, 3)],
+            [(None, GGR.at[pl.ds(base, 3)])],
         )
 
-    def gain_sum(a, tot):
-        for k in range(3):
-            tot = tot + GGR[base + 3 * a + k]
+    def gain_sum(lo, hi, tot):
+        for k in range(lo, hi):
+            tot = tot + GGR[k]
         return tot
-
-    gs = gain_step(0, "z")
-    add_phase("4", 1, s4)
-    s4 = sum_phase("4", 0)
-    arrived(gs)
-    tot = gain_sum(0, tot)
-    gs = gain_step(1, "y")
-
-    add_phase("1a", 2, s1a)
-    s1a = sum_phase("1a", 1)
-    add_phase("1b", 2, s1b)
-    s1b = sum_phase("1b", 1)
 
     def into(k):
         def out(v):
@@ -783,23 +802,49 @@
     def out_4(v):
         c4f[...] = v.reshape(16, 384)
 
+    def out_down(v):
+        MISC[0:16, :] = v.reshape(16, 640)
+
+    add_phase("4", 2, s4)
+    s4 = sum_phase("4", 1)
+    add_phase("1b", 2, s1b)
+    s1b = sum_phase("1b", 1)
+    add_phase("1a", 2, s1a)
+    s1a = sum_phase("1a", 1)
     arrived(gs)
-    tot = gain_sum(1, tot)
-    gs = gain_step(2, "x")
+    tot = gain_sum(0, 7, GG[...])
+    gs = gain_step("z", 7, tot)
+    add_phase("4", 1, s4)
+    s4 = sum_phase("4", 0)
+    add_phase("5", 0, s5, out_down)
     add_phase("2", 0, s2, into(1))
     add_phase("3", 0, s3, into(2))
-    add_phase("4", 0, s4, out_4)
-    pair = send(c4f.at[pl.ds(pl.multiple_of(8 * (1 - y % 2), 8), 8), :], R4, near_y())
     for e in range(16):
         for k in (1, 2):
             F2[e, 5 * k:5 * k + 5, :] = mf[k, 5 * e:5 * e + 5, :]
+    add_phase("1b", 1, s1b)
     add_phase("1a", 1, s1a)
-    add_phase("1b", 1, s1b)
     s1 = sum_phase("1", 0)
     arrived(gs)
-    tot = gain_sum(2, tot)
+    tot = gain_sum(7, 10, tot)
+    gs = gain_step("x", 11, tot)
+    add_phase("4", 0, s4, out_4)
+    pair = send(c4f.at[pl.ds(pl.multiple_of(8 * (1 - y % 2), 8), 8), :], R4, near_y())
+    add_phase("1", 0, s1, into(0))
+    for e in range(16):
+        F2[e, 0:5, :] = mf[0, 5 * e:5 * e + 5, :]
+    earlier = list(sent)
+    sent.clear()
+    home = post(
+        [(None, F2.at[(j // 4) % 2 * 8 + j // 8 * 4 + j % 4], o_cols.at[gi], member(j)) for j in others],
+        [(None, o_cols.at[pl.ds(0, 15)])],
+    )
+    keep_cols = pltpu.make_async_copy(F2.at[ge], o_cols.at[gi], ls)
+    keep_cols.start()
+    MISC[24:32, :] = jnp.zeros((8, D), F32)
+    arrived(gs)
+    tot = gain_sum(11, 14, tot)
     shard = f * 4 + y
-    MISC[24:32, :] = jnp.zeros((8, D), F32)
     for k, (_, per, width) in enumerate(GAINS):
         line = tot[k:k + 1, 0:width]
         col = iota((1, width), 1)
@@ -810,19 +855,11 @@
     left = y % 2 == 0
     MISC[16:24, 0:384] = jnp.where(left, own, R4[...])
     MISC[16:24, 384:640] = jnp.where(left, R4[...], own)[:, 0:256]
+    keep_cols.wait()
     keep_rows = pltpu.make_async_copy(MISC, o_rows, ls)
     keep_rows.start()
+    all_gone(earlier)
     keep_rows.wait()
-    add_phase("1", 0, s1, into(0))
-    for e in range(16):
-        F2[e, 0:5, :] = mf[0, 5 * e:5 * e + 5, :]
-    home = post(
-        [(None, F2.at[(j // 4) % 2 * 8 + j // 8 * 4 + j % 4], o_cols.at[gi], member(j)) for j in others],
-        [(None, o_cols.at[pl.ds(0, 15)])],
-    )
-    keep_cols = pltpu.make_async_copy(F2.at[ge], o_cols.at[gi], ls)
-    keep_cols.start()
-    keep_cols.wait()
     arrived(gx_in + lo_in + home)
     all_gone(sent)
 
@@ -875,7 +912,7 @@
         b(3, 1, 1, 48, 512), b(3, 1, 1, 32, 512), b(3, 1, 1, 80, 512), b(3, 1, 1, 80, 512),
         b(3, 1, 4, 1, 16, 384), b(3, 4, 1, 1, 16, 640),
         b(3, 1, 1, 80, 128), b(3, 1, 1, 80, 128), b(3, 1, 1, 80, 128), b(3, 1, 1, 1, 16, 384), b(3, 1, 1, 1, 16, 640),
-        v(8, D), v(13, 8, D), v(16, 16, 128), v(16, 384), v(8, 384), v(32, D),
+        v(8, D), v(15, 8, D), v(16, 16, 128), v(16, 384), v(8, 384), v(32, D),
         pltpu.SemaphoreType.DMA((N_SEM,)), pltpu.SemaphoreType.DMA((N_SEM,)), pltpu.SemaphoreType.DMA,
     ]
     return out

time: 140 us -> 133 us (0.950)
  Pallas kernels: 138 us -> 132 us
    pallas_call x1, Pallas kernels: 136 us -> 129 us  [on_device(): pl.pallas_call(kernel, out_shape=(s(2, 256, D, dtype=BF), s(2, 256, D, dt...]
where the time goes in v3:
time: 133 us
  Pallas kernels  132 us (99%)
    pallas_call x1, Pallas kernels, on_device(): pl.pallas_call(kernel, out_shape=(s(2, 256, D, dtype=BF), s(2, 256, D, dt...  129 us
    pallas_call x1, Pallas kernels, on_device(): pl.pallas_call(finish, out_shape=(s(2, 256, D, dtype=BF), s(2, 256, D), s...  2.77 us

profile of v3, /device:TPU:1, one launch (start us, length us, event | category | flops | bytes accessed | tf_op | source)
XLA Modules:
  0.0 132.6 jit_solution(6325482862938942986)
XLA Ops:
  0.7 129.0 %block.1 = (bf16[2,256,640]{2,1,0:T(8,128)(2,1)}, bf16[2,256,640]{2,1,0:T(8,128)(2,1)}, f32[16,16,128]{2,1,0:T(8,128)}, f32[32,640]{1,0:T(8,128)}) custom-call(bf16[2,256,640]{2,1,0:T(8,128)(2,1)} %tok.1, bf16[2,256,640]{2,1,0:T(8,128)(2,1)} %cot.1, s32[1,2,3]{2,1,0:T(2,128)} %dl.1, bf16[1,5]{1,0:T(2,128)(2,1)} %bitcast.12, bf16[1,5]{1,0:T(2,128)(2,1)} %bitcast.13, ...), custom_call_target="tpu_custom_call" | custom-call | tf_op jit(solution)/shard_map/block/pallas_call | solution.py:930
  129.7 2.8 %finish.1 = (bf16[2,256,640]{2,1,0:T(8,128)(2,1)}, f32[2,256,640]{2,1,0:T(8,128)}, f32[5,1024]{1,0:T(8,128)}, f32[5,256]{1,0:T(8,128)}, f32[5,256]{1,0:T(8,128)}...) custom-call(bf16[2,256,640]{2,1,0:T(8,128)(2,1)} %get-tuple-element., ...), custom_call_target="tpu_custom_call" | custom-call | tf_op jit(solution)/shard_map/finish/pallas_call | solution.py:941

commit v4 on v3

--- a/solution.py
+++ b/solution.py
@@ -708,14 +708,10 @@
             add_phase("2", 2, s2)
             held["2"] = sum_phase("2", 1)
 
-        steps = {0: early} if s == 0 else {2: one}
+        steps = {} if s == 0 else {1: early, 2: one}
         lax.fori_loop(0, blocks[s] + 1, functools.partial(backward, progress=steps), 0)
-        if s == 0:
-            s4 = held["4"]
-            add_phase("5", 2, s5)
-            s5 = sum_phase("5", 1)
-        else:
-            s2 = held["2"]
+        if s == 1:
+            s2, s4 = held["2"], held["4"]
 
         def query_back(h, carry, s=s):
             dq = turn_back(OA[h] * 0.0625, CS[s], SN[s])
@@ -737,6 +733,8 @@
     s1 = sum_core("1", 0)
     add_phase("3", 2, s3)
     s3 = sum_phase("3", 1)
+    add_phase("5", 2, s5)
+    s5 = sum_phase("5", 1)
     arrived(dk_cp)
     for s in range(2):
         r = slice(256 * s, 256 * s + 256)

time: 133 us -> 132 us (level)
  no operation moved by 1% of the time
where the time goes in v4:
time: 132 us
  Pallas kernels  131 us (99%)
    pallas_call x1, Pallas kernels, on_device(): pl.pallas_call(kernel, out_shape=(s(2, 256, D, dtype=BF), s(2, 256, D, dt...  129 us
    pallas_call x1, Pallas kernels, on_device(): pl.pallas_call(finish, out_shape=(s(2, 256, D, dtype=BF), s(2, 256, D), s...  2.77 us

profile of v4, /device:TPU:1, one launch (start us, length us, event | category | flops | bytes accessed | tf_op | source)
XLA Modules:
  0.0 132.2 jit_solution(4024520679233070224)
XLA Ops:
  0.7 128.6 %block.1 = (bf16[2,256,640]{2,1,0:T(8,128)(2,1)}, bf16[2,256,640]{2,1,0:T(8,128)(2,1)}, f32[16,16,128]{2,1,0:T(8,128)}, f32[32,640]{1,0:T(8,128)}) custom-call(bf16[2,256,640]{2,1,0:T(8,128)(2,1)} %tok.1, bf16[2,256,640]{2,1,0:T(8,128)(2,1)} %cot.1, s32[1,2,3]{2,1,0:T(2,128)} %dl.1, bf16[1,5]{1,0:T(2,128)(2,1)} %bitcast.12, bf16[1,5]{1,0:T(2,128)(2,1)} %bitcast.13, ...), custom_call_target="tpu_custom_call" | custom-call | tf_op jit(solution)/shard_map/block/pallas_call | solution.py:928
  129.2 2.8 %finish.1 = (bf16[2,256,640]{2,1,0:T(8,128)(2,1)}, f32[2,256,640]{2,1,0:T(8,128)}, f32[5,1024]{1,0:T(8,128)}, f32[5,256]{1,0:T(8,128)}, f32[5,256]{1,0:T(8,128)}...) custom-call(bf16[2,256,640]{2,1,0:T(8,128)(2,1)} %get-tuple-element., ...), custom_call_target="tpu_custom_call" | custom-call | tf_op jit(solution)/shard_map/finish/pallas_call | solution.py:939
